TPU v7x, 256 devices: a whole 4x4x8 slice. The times are simulated.
256 devices in a mesh: rep: 16 (over x, z_lo, core), fsdp: 16 (over y, z_hi).
Axes of the slice: x: 4, y: 4, z: 8 (z_hi: 4, z_lo: 2; z = z_hi * 2 + z_lo), core: 2. Of those that a mesh axis runs over, the one named last changes fastest.
Arguments:
- tokens: bfloat16 [131072, 2560], P(('rep', 'fsdp')), may hold values from -6 to 6
- out_grads: bfloat16 [131072, 4096], P(('rep', 'fsdp')), may hold values from -0.625 to 0.625
- weight: bfloat16 [4096, 2560], P('fsdp'), may hold values from -0.75 to 0.75
- momentum: bfloat16 [16, 4096, 2560], P('rep', 'fsdp'), may hold values from -6 to 6
- kept_blocks: int32 [16, 64, 40, 4], P('rep', 'fsdp'), may hold values from 0 to 63, as said below
Outputs:
- new_weight: bfloat16 [4096, 2560], P('fsdp')
- new_momentum: bfloat16 [16, 4096, 2560], P('rep', 'fsdp')
Inputs may be any that keep to these rules, and one draw needn't show every extreme that they name: `kept_blocks`: the 4 block numbers of each span of each replica are distinct.
All inputs are finite; a program needn't handle non-finite values.
Results may differ from a plain program's by a relative error of at most 0.015.
Values may be sent and summed in bfloat16 or wider, within the bound.
A program may use at most 128 MiB of HBM per device.

v0:
```python
import jax
import jax.numpy as jnp
from jax import lax
from jax.sharding import PartitionSpec as P

beta_decay = 0.9
step_rate = 0.5


def dct_table():
    position = jnp.arange(64, dtype=jnp.float32)
    frequency = position[:, None]
    scaling = jnp.where(frequency == 0, jnp.sqrt(1.0 / 64.0), jnp.sqrt(2.0 / 64.0))
    return scaling * jnp.cos(jnp.pi * (2.0 * position[None, :] + 1.0) * frequency / 128.0)


def to_cells(field, row_blocks, col_blocks):
    shaped = field.reshape(row_blocks, 64, col_blocks, 64)
    return shaped.transpose(1, 3, 0, 2).reshape(64, 64, row_blocks * col_blocks)


def from_cells(cells, row_blocks, col_blocks):
    shaped = cells.reshape(64, 64, row_blocks, col_blocks)
    return shaped.transpose(2, 0, 3, 1).reshape(row_blocks * 64, col_blocks * 64)


def forward(cells, cosine_table):
    halfway = jnp.einsum("ki,ijc->kjc", cosine_table, cells, precision=lax.Precision.HIGHEST)
    spectra = jnp.einsum("lj,kjc->klc", cosine_table, halfway, precision=lax.Precision.HIGHEST)
    spans = spectra.shape[2]
    return spectra.reshape(8, 8, 8, 8, spans).transpose(0, 2, 1, 3, 4).reshape(64, 64, spans)


def inverse(blocked, cosine_table):
    spans = blocked.shape[2]
    spectra = blocked.reshape(8, 8, 8, 8, spans).transpose(0, 2, 1, 3, 4).reshape(64, 64, spans)
    halfway = jnp.einsum("ki,klc->ilc", cosine_table, spectra, precision=lax.Precision.HIGHEST)
    return jnp.einsum("lj,ilc->ijc", cosine_table, halfway, precision=lax.Precision.HIGHEST)


def block_mask(chosen):
    numbers = jnp.arange(64, dtype=jnp.int32)
    return (chosen[None, :, :] == numbers[:, None, None]).astype(jnp.float32)


def pick_blocks(blocked, chosen):
    return jnp.einsum("bkc,bwc->kwc", block_mask(chosen), blocked, precision=lax.Precision.HIGHEST)


def place_blocks(picked, chosen):
    return jnp.einsum("bkc,kwc->bwc", block_mask(chosen), picked, precision=lax.Precision.HIGHEST)


def shards(tokens, out_grads, weight, momentum, kept_blocks):
    shard_rows = weight.shape[0]
    width = weight.shape[1]
    row_blocks = shard_rows // 64
    col_blocks = width // 64
    span_count = row_blocks * col_blocks
    cosine_table = dct_table()
    gradient = lax.psum_scatter(
        lax.dot_general(
            out_grads, tokens, (((0,), (0,)), ((), ())), preferred_element_type=jnp.float32
        ).astype(jnp.bfloat16),
        "fsdp",
        scatter_dimension=0,
        tiled=True,
    ).astype(jnp.float32)
    moment = beta_decay * momentum[0].astype(jnp.float32) + gradient
    blocked = forward(to_cells(moment, row_blocks, col_blocks), cosine_table)
    chosen = kept_blocks.reshape(span_count, kept_blocks.shape[3]).T
    picked = pick_blocks(blocked, chosen)
    own_sparse = place_blocks(picked, chosen)
    removed = from_cells(inverse(own_sparse, cosine_table), row_blocks, col_blocks)
    new_momentum = (moment - removed).astype(jnp.bfloat16)[None]
    replica_count = lax.axis_size("rep")
    empty_cells = jnp.zeros((64, 64, span_count), jnp.float32)
    peer_picked = lax.all_gather(
        picked[None].astype(jnp.bfloat16), "rep", axis=0, tiled=True
    ).astype(jnp.float32)
    peer_chosen = lax.all_gather(chosen[None], "rep", axis=0, tiled=True)
    numbers = jnp.arange(64, dtype=jnp.int32)
    masks = (peer_chosen[:, None, :, :] == numbers[None, :, None, None]).astype(jnp.float32)
    summed_coeffs = empty_cells + jnp.einsum(
        "rbkc,rkwc->bwc", masks, peer_picked, precision=lax.Precision.HIGHEST
    )
    decoded = inverse(summed_coeffs, cosine_table)
    update = from_cells(decoded, row_blocks, col_blocks) / replica_count
    new_weight = (weight.astype(jnp.float32) - step_rate * update).astype(jnp.bfloat16)
    return (new_weight, new_momentum)


def solution(mesh):
    placed = (
        P(("rep", "fsdp"), None),
        P(("rep", "fsdp"), None),
        P("fsdp", None),
        P("rep", "fsdp", None),
        P("rep", "fsdp", None, None),
    )
    return jax.shard_map(
        shards,
        mesh=mesh,
        in_specs=placed,
        out_specs=(P("fsdp", None), P("rep", "fsdp", None)),
        check_vma=False,
    )
```

profile of v0, /device:TPU:1, one launch (start us, length us, event | category | flops | bytes accessed | tf_op | source)
XLA Modules:
  0.0 453.1 jit_solution(3757126857353779202)
XLA Ops:
  7.2 0.0 copy-start
  7.2 0.0 reduce-scatter.2.cloned.1.call-start
  7.2 1.7 copy-done
  8.9 17.7 %convolution_convert_fusion = bf16[4096,2560]{1,0:T(8,128)(2,1)} fusion(bf16[512,4096]{1,0:T(8,128)(2,1)} %param.6, bf16[512,2560]{1,0:T(8,128)(2,1)S(1)} %copy-done), kind=kOutput, calls=%fused_computation | convolution fusion | flops 10747904000 | bytes 27787264 | tf_op jit(solution)/shard_map/dot_general | solution.py:62
  26.6 0.0 copy-start.2
  26.6 0.0 reduce-scatter.2.cloned.1.call-update
  26.6 0.3 all-gather.5.cloned.1.call-start
  26.9 0.4 copy-done.2
  27.3 0.1 reshape.69
  27.4 0.1 copy.105
  27.5 252.7 %reduce-scatter.2.cloned.1.call-done = bf16[256,2560]{1,0:T(8,128)(2,1)} async-done(((bf16[4096,2560]{1,0:T(8,128)(2,1)}), bf16[256,2560]{1,0:T(8,128)(2,1)}) %reduce-scatter.2.cloned.1.call-update) | async-done | bytes 1310736 | tf_op jit(solution)/shard_map/reduce_scatter | solution.py:61
  280.2 2.1 bitcast_add_fusion
  282.3 2.9 reshape.65
  285.2 5.5 %copy.98 = f32[4,64,40,64]{3,2,0,1:T(8,128)} copy(f32[4,64,40,64]{3,2,1,0:T(8,128)} %reshape.65) | data formatting | bytes 5242880 | tf_op jit(solution)/shard_map/reshape | solution.py:18
  290.7 6.5 %copy.100 = f32[64,64,160]{2,0,1:T(8,128)} copy(f32[64,64,160]{1,2,0:T(8,128)} %bitcast.73) | data formatting | bytes 5242880 | tf_op jit(solution)/shard_map/reshape | solution.py:19
  297.3 5.8 %fusion.23 = f32[64,64,160]{2,0,1:T(8,128)S(1)} fusion(f32[64,64,160]{2,0,1:T(8,128)} %copy.100, f32[64]{0:T(128)S(1)} %get-tuple-element.3, f32[64]{0:T(128)S(1)} %get-tuple-element.2), kind=kOutput, calls=%fused_computation.27 | convolution fusion | flops 503328768 | bytes 5243392 | tf_op jit(solution)/shard_map/ki,ijc->kjc/dot_general | solution.py:28
  303.1 6.6 %fusion.9 = f32[64,160,64]{1,2,0:T(8,128)S(1)} fusion(f32[64,64,160]{2,0,1:T(8,128)S(1)} %fusion.23, f32[64]{0:T(128)S(1)} %get-tuple-element.3, f32[64]{0:T(128)S(1)} %get-tuple-element.2), kind=kOutput, calls=%fused_computation.11 | convolution fusion | flops 503328768 | bytes 5243392 | tf_op jit(solution)/shard_map/lj,kjc->klc/dot_general | solution.py:29
  309.6 2.6 copy.103
  312.3 6.6 %copy.106 = f32[64,64,160]{1,0,2:T(8,128)} copy(f32[64,64,160]{2,1,0:T(8,128)} %bitcast.77) | data formatting | bytes 5242880 | tf_op jit(solution)/shard_map/reshape | solution.py:31
  318.9 5.1 %fusion.19 = f32[160,64,4]{1,2,0:T(4,128)S(1)} fusion(f32[64,64,160]{1,0,2:T(8,128)} %copy.106, s32[4,160]{0,1:T(8,128)S(1)} %copy.105), kind=kOutput, calls=%fused_computation.23 | convolution fusion | flops 31498240 | bytes 2787840 | tf_op jit(solution)/shard_map/bkc,bwc->kwc/dot_general | solution.py:47
  323.9 0.2 copy.107
  324.1 0.7 bitcast_convert_fusion
  324.8 0.0 all-gather.5.cloned.1.call-update
  324.8 19.1 %all-gather.2 = s32[16,4,160]{2,1,0:T(4,128)S(1)} all-gather(s32[1,4,160]{2,1,0:T(4,128)S(1)} %bitcast.85), channel_id=3, replica_groups=mesh['rep'=16,'fsdp'=16] {'rep'}, dimensions={0}, use_global_device_ids=true | all-gather | bytes 43520 | tf_op jit(solution)/shard_map/all_gather | solution.py:81
  344.0 0.2 copy.108
  344.2 0.2 copy.116
  344.4 6.2 %convolution_bitcast_fusion = f32[64,64,160]{0,1,2:T(8,128)} fusion(f32[4,64,160]{1,0,2:T(4,128)S(1)} %copy.116, s32[4,160]{0,1:T(8,128)S(1)} %copy.105), kind=kOutput, calls=%fused_computation.18 | convolution fusion | flops 31498240 | bytes 2787840 | tf_op jit(solution)/shard_map/bkc,kwc->bwc/dot_general | solution.py:51
  350.6 7.1 %copy.117 = f32[64,64,160]{2,1,0:T(8,128)} copy(f32[64,64,160]{0,1,2:T(8,128)} %convolution_bitcast_fusion) | data formatting | bytes 5242880 | tf_op jit(solution)/shard_map/bkc,kwc->bwc/transpose | solution.py:51
  357.7 2.8 copy.118
  360.5 6.4 %fusion.3 = f32[64,64,160]{2,0,1:T(8,128)S(1)} fusion(f32[64,64,160]{2,1,0:T(8,128)S(1)} %bitcast.79, f32[64]{0:T(128)S(1)} %get-tuple-element.3, f32[64]{0:T(128)S(1)} %get-tuple-element.2), kind=kOutput, calls=%fused_computation.5 | convolution fusion | flops 503328768 | bytes 5243392 | tf_op jit(solution)/shard_map/ki,klc->ilc/dot_general | solution.py:37
  366.9 7.6 %fusion.15 = f32[64,64,160]{2,1,0:T(8,128)} fusion(f32[64,64,160]{2,0,1:T(8,128)S(1)} %fusion.3, f32[64]{0:T(128)S(1)} %get-tuple-element.3, f32[64]{0:T(128)S(1)} %get-tuple-element.2), kind=kOutput, calls=%fused_computation.20 | convolution fusion | flops 503328768 | bytes 5243392 | tf_op jit(solution)/shard_map/lj,ilc->ijc/dot_general | solution.py:38
  374.6 5.8 %copy.121 = f32[64,64,160]{1,2,0:T(8,128)} copy(f32[64,64,160]{2,1,0:T(8,128)} %fusion.15) | data formatting | bytes 5242880 | tf_op jit(solution)/shard_map/lj,ilc->ijc/transpose | solution.py:38
  380.4 5.2 %copy.122 = f32[4,64,40,64]{3,2,1,0:T(8,128)} copy(f32[4,64,40,64]{3,2,0,1:T(8,128)} %bitcast.74) | data formatting | bytes 5242880 | tf_op jit(solution)/shard_map/transpose | solution.py:24
  385.5 3.8 reshape.75
  389.3 3.3 fusion.18
  392.6 0.0 all-gather.5.cloned.1.call-done
  392.6 3.9 copy.109
  396.6 5.8 %fusion.12 = f32[64,64,160]{0,1,2:T(8,128)} fusion(bf16[16,4,64,160]{2,0,1,3:T(8,128)(2,1)S(1)} %copy.109, s32[16,4,160]{0,1,2:T(4,128)S(1)} %copy.108), kind=kOutput, calls=%fused_computation.19 | convolution fusion | flops 84541440 | bytes 3973120 | tf_op jit(solution)/shard_map/rbkc,rkwc->bwc/dot_general | solution.py:84
  402.4 7.3 %copy.110 = f32[64,64,160]{2,1,0:T(8,128)} copy(f32[64,64,160]{0,1,2:T(8,128)} %fusion.12) | data formatting | bytes 5242880 | tf_op jit(solution)/shard_map/rbkc,rkwc->bwc/transpose | solution.py:84
  409.7 2.8 copy.111
  412.5 6.4 %fusion.7 = f32[64,64,160]{2,0,1:T(8,128)S(1)} fusion(f32[64,64,160]{2,1,0:T(8,128)S(1)} %bitcast.81, f32[64]{0:T(128)S(1)} %get-tuple-element.3, f32[64]{0:T(128)S(1)} %get-tuple-element.2), kind=kOutput, calls=%fused_computation.9 | convolution fusion | flops 503328768 | bytes 5243392 | tf_op jit(solution)/shard_map/ki,klc->ilc/dot_general | solution.py:37
  418.9 7.5 %multiply_bitcast_fusion = f32[64,64,160]{2,1,0:T(8,128)} fusion(f32[64,64,160]{2,0,1:T(8,128)S(1)} %fusion.7, f32[64]{0:T(128)S(1)} %get-tuple-element.3, f32[64]{0:T(128)S(1)} %get-tuple-element.2), kind=kOutput, calls=%fused_computation.13 | convolution fusion | flops 503984128 | bytes 5243392 | tf_op jit(solution)/shard_map/lj,ilc->ijc/dot_general | solution.py:38
  426.4 5.8 %copy.114 = f32[64,64,160]{1,2,0:T(8,128)} copy(f32[64,64,160]{2,1,0:T(8,128)} %multiply_bitcast_fusion) | data formatting | bytes 5242880 | tf_op jit(solution)/shard_map/mul | solution.py:89
  432.2 5.2 %copy.115 = f32[4,64,40,64]{3,2,1,0:T(8,128)} copy(f32[4,64,40,64]{3,2,0,1:T(8,128)} %bitcast.75) | data formatting | bytes 5242880 | tf_op jit(solution)/shard_map/mul | solution.py:89
  437.4 0.0 copy-start.1
  437.4 5.2 %mul.157 = f32[256,2560]{1,0:T(8,128)} reshape(f32[4,64,40,64]{3,2,1,0:T(8,128)} %copy.115) | data formatting | bytes 5242880 | tf_op jit(solution)/shard_map/mul | solution.py:89
  442.6 3.5 subtract_convert_fusion.1
  446.0 0.0 copy-done.1
  (2 shorter events, 0.0 us)
Async XLA Ops:
  7.2 1.7 copy-start
  7.2 273.0 %reduce-scatter.2.cloned.1.call-start = ((), (), s32[]{:S(2)}) async-start(), calls=%async_computation.1 | async-start | bytes 22282240 | tf_op jit(solution)/shard_map/reduce_scatter | solution.py:61
  26.6 0.7 copy-start.2
  26.6 366.0 %all-gather.5.cloned.1.call-start = ((), (), s32[]{:S(2)}) async-start(), calls=%async_computation.2 | async-start | bytes 2228224 | tf_op jit(solution)/shard_map/all_gather | solution.py:78
  437.4 8.7 %copy-start.1 = (bf16[512,2560]{1,0:T(8,128)(2,1)S(1)}, bf16[512,2560]{1,0:T(8,128)(2,1)}, u32[]{:S(2)}) copy-start(bf16[512,2560]{1,0:T(8,128)(2,1)} %param.5) | copy-start | bytes 7864324
Sparse Core Ops, SparseCore 0:
  26.7 253.4 reduce-scatter.1
  325.0 35.0 all-gather.4
where the time goes:
time: 459 us; the launch traced here: 453 us
  waiting for transfers between devices  253 us (55%)
  local copies, waits for them, and re-layouts  81.9 us (18%)
  matrix products  75.1 us (16%)
  blocking collectives  19.1 us (4%)
  between operations  14.4 us (3%)
  other arithmetic  9.55 us (2%)
    reduce_scatter x1, waiting for transfers between devices, shards(): lax.psum_scatter(lax.dot_general(out_grads, tokens, (((0,), (0,)), ((), (...  253 us
    all_gather x1, blocking collectives, shards(): peer_chosen = lax.all_gather(chosen[None], 'rep', axis=0, tiled=True)  19.1 us
    dot_general x1, matrix products, shards(): lax.dot_general(out_grads, tokens, (((0,), (0,)), ((), ())), preferred_el...  17.7 us
    mul x3, local copies, waits for them, and re-layouts, shards(): step_rate * update  16.2 us
    dot_general x2, matrix products, inverse(): jnp.einsum('lj,ilc->ijc', cosine_table, halfway, precision=lax.Precision....  15.1 us
    dot_general x2, matrix products, inverse(): jnp.einsum('ki,klc->ilc', cosine_table, spectra, precision=lax.Precision....  12.8 us
    reshape x2, local copies, waits for them, and re-layouts, forward(): spectra.reshape(8, 8, 8, 8, spans).transpose(0, 2, 1, 3, 4)  9.24 us
  transfers between devices with their start and end apart: 2, of which 1 were waited for; matrix products, arithmetic and copies ran while one was open for 11% of the time, Pallas kernels for 0%

commit v1 on v0

v1 whole, which is shorter than its diff:
```python
import functools

import jax
import jax.numpy as jnp
import numpy as np
from jax import lax
from jax.experimental import pallas as pl
from jax.experimental.pallas import tpu as pltpu
from jax.sharding import PartitionSpec as P

beta_decay = 0.9
step_rate = 0.5

MESH = pl.DeviceIdType.MESH
F32 = jnp.float32
BF16 = jnp.bfloat16

D = 2560
ROWS = 256
SIDE = 4
REPS = 16

JOBS = (
    ("y", 0, 1024, 256),
    ("y", 256, 1280, 256),
    ("y", 512, 1536, 256),
    ("y", 768, 1792, 128),
    ("y", 896, 1920, 128),
    ("z", 2048, 2304, 256),
)
ORDER = (
    (0, 0), (0, 5), (1, 0), (0, 1), (1, 5), (2, 0), (1, 1), (0, 2), (2, 1), (2, 5),
    (1, 2), (0, 3), (3, 0), (2, 2), (1, 3), (0, 4), (3, 5), (3, 1), (4, 0), (2, 3),
    (1, 4), (4, 5), (4, 1), (3, 2), (2, 4), (3, 3), (4, 2), (3, 4), (4, 3), (4, 4),
)


def scatter_kernel(g_hbm, t_ref, out_ref, gt, stage, load_sem, send_sem, recv_sem, *bufs):
    wide, thin = bufs[: len(JOBS)], bufs[len(JOBS) :]
    rep = lax.axis_index("rep")
    member = lax.axis_index("fsdp")
    pos = {"y": member // SIDE, "z": member % SIDE}

    def device(axis, index):
        if axis == "y":
            return (rep, index * SIDE + pos["z"])
        return (rep, pos["y"] * SIDE + index)

    def turn(index, by):
        return lax.rem(index + (by + SIDE), SIDE)

    loads = []
    for block in range(SIDE):
        group = turn(pos["y"], 2 + block)
        loads.append(
            pltpu.make_async_copy(
                g_hbm.at[:, pl.ds(pl.multiple_of(group * 1024, 1024), 1024)],
                stage.at[block],
                load_sem.at[block],
            )
        )
        loads[-1].start()

    barrier = pltpu.get_barrier_semaphore()
    for axis in ("y", "z"):
        for by in (1, -1):
            pl.semaphore_signal(
                barrier, inc=1, device_id=device(axis, turn(pos[axis], by)), device_id_type=MESH
            )
    pl.semaphore_wait(barrier, 4)

    for block in range(SIDE):
        group = turn(pos["y"], 2 + block)
        loads[block].wait()

        @pl.loop(0, SIDE)
        def _(part, block=block, group=group):
            start = pl.multiple_of(group * 1024 + part * ROWS, ROWS)
            gt[pl.ds(start, ROWS), :] = stage[
                block, :, pl.ds(pl.multiple_of(part * ROWS, ROWS), ROWS)
            ].T

    def partial(axis, group, other, column, width):
        owner = group * SIDE + other if axis == "y" else other * SIDE + group
        rows = pl.ds(pl.multiple_of(owner * ROWS, ROWS), ROWS)
        return jnp.dot(
            gt[rows, :], t_ref[:, column : column + width], preferred_element_type=F32
        )

    sent = []

    def send(src, dst, job, side, number, target):
        copy = pltpu.make_async_remote_copy(
            src_ref=src,
            dst_ref=dst,
            send_sem=send_sem.at[job, side, number],
            recv_sem=recv_sem.at[job, side, number],
            device_id=target,
            device_id_type=MESH,
        )
        copy.start()
        sent.append(copy)

    def arrived(dst, job, side, number):
        pltpu.make_async_remote_copy(
            src_ref=dst,
            dst_ref=dst,
            send_sem=send_sem.at[job, side, number],
            recv_sem=recv_sem.at[job, side, number],
            device_id=(rep, member),
            device_id_type=MESH,
        ).wait_recv()

    for step, job in ORDER:
        axis, column_a, column_b, width = JOBS[job]
        other_axis = "z" if axis == "y" else "y"
        m, n = pos[axis], pos[other_axis]
        sides = ((0, column_a, -1), (1, column_b, 1))
        if step == 0:
            for slot in (0, 1):
                for side, column, d in sides:
                    buf = wide[job].at[side]
                    group, target = (turn(m, 2), turn(m, d)) if slot == 0 else (turn(m, -d),) * 2

                    @pl.loop(0, SIDE)
                    def _(other, buf=buf, group=group, column=column, slot=slot):
                        buf[slot, other] = partial(axis, group, other, column, width).astype(BF16)

                    send(buf.at[slot], buf.at[slot + 2], job, side, slot, device(axis, target))
        elif step == 1:
            for side, column, d in sides:
                buf = wide[job].at[side]
                arrived(buf.at[2], job, side, 0)

                @pl.loop(0, SIDE)
                def _(other, buf=buf, group=turn(m, d), column=column):
                    total = partial(axis, group, other, column, width) + buf[2, other].astype(F32)
                    buf[2, other] = total.astype(BF16)

                send(buf.at[2], buf.at[4], job, side, 2, device(axis, turn(m, d)))
        elif step == 2:
            for side, column, d in sides:
                buf, low = wide[job].at[side], thin[job].at[side]
                arrived(buf.at[3], job, side, 1)
                arrived(buf.at[4], job, side, 2)
                for slot, other in ((0, turn(n, 2)), (1, turn(n, -d)), (2, turn(n, d)), (3, n)):
                    total = (
                        partial(axis, m, other, column, width)
                        + buf[3, other].astype(F32)
                        + buf[4, other].astype(F32)
                    )
                    if slot == 3:
                        out_ref[:, column : column + width] = total
                    else:
                        low[slot] = total.astype(BF16)
                    if slot < 2:
                        target = turn(n, d) if slot == 0 else turn(n, -d)
                        send(
                            low.at[slot],
                            low.at[slot + 3],
                            job,
                            side,
                            slot + 3,
                            device(other_axis, target),
                        )
        elif step == 3:
            for side, column, d in sides:
                low = thin[job].at[side]
                arrived(low.at[3], job, side, 3)
                low[3] = (low[2].astype(F32) + low[3].astype(F32)).astype(BF16)
                send(low.at[3], low.at[5], job, side, 5, device(other_axis, turn(n, d)))
        else:
            for side, column, d in sides:
                low = thin[job].at[side]
                arrived(low.at[4], job, side, 4)
                arrived(low.at[5], job, side, 5)
                out_ref[:, column : column + width] += low[4].astype(F32) + low[5].astype(F32)

    for copy in sent:
        copy.wait_send()


def reduced_gradient(out_grads, tokens):
    vmem = pl.BlockSpec(memory_space=pltpu.VMEM)
    return pl.pallas_call(
        scatter_kernel,
        out_shape=jax.ShapeDtypeStruct((ROWS, D), F32),
        in_specs=[pl.BlockSpec(memory_space=pl.ANY), vmem],
        out_specs=vmem,
        scratch_shapes=[
            pltpu.VMEM((4096, 512), BF16),
            pltpu.VMEM((SIDE, 512, 1024), BF16),
            pltpu.SemaphoreType.DMA((SIDE,)),
            pltpu.SemaphoreType.DMA((len(JOBS), 2, 6)),
            pltpu.SemaphoreType.DMA((len(JOBS), 2, 6)),
        ]
        + [pltpu.VMEM((2, 5, SIDE, ROWS, job[3]), BF16) for job in JOBS]
        + [pltpu.VMEM((2, 6, ROWS, job[3]), BF16) for job in JOBS],
        compiler_params=pltpu.CompilerParams(
            collective_id=0, has_side_effects=True, vmem_limit_bytes=60 * 2**20
        ),
        cost_estimate=pl.CostEstimate(
            flops=2 * 512 * 4096 * D, bytes_accessed=2 * 512 * (4096 + D), transcendentals=0
        ),
    )(out_grads, tokens)


def split_dot(left, right):
    total = jnp.dot(left[0], right[0], preferred_element_type=F32)
    total += jnp.dot(left[0], right[1], preferred_element_type=F32)
    return total + jnp.dot(left[1], right[0], preferred_element_type=F32)


def halves(value):
    high = value.astype(BF16)
    return high, (value - high.astype(F32)).astype(BF16)


def codec_kernel(
    grad_ref, mom_ref, own_ref, kept_ref, weight_ref, table_ref, fold_ref, spread_ref,
    new_weight_ref, new_mom_ref,
    picked, packed, packed_in, kept_in, tile,
    kept_send, kept_recv, pack_send, pack_recv, tile_send, tile_recv,
):
    rep = lax.axis_index("rep")
    member = lax.axis_index("fsdp")

    def peer(by):
        return lax.rem(rep + by, REPS)

    barrier = pltpu.get_barrier_semaphore()
    for by in range(1, REPS):
        pl.semaphore_signal(barrier, inc=1, device_id=(peer(by), member), device_id_type=MESH)
    pl.semaphore_wait(barrier, REPS - 1)

    def copy_to(src, dst, send_sem, recv_sem, target):
        return pltpu.make_async_remote_copy(
            src_ref=src, dst_ref=dst, send_sem=send_sem, recv_sem=recv_sem,
            device_id=(target, member), device_id_type=MESH,
        )

    sent = []
    for by in range(1, REPS):
        copy = copy_to(
            kept_ref.at[peer(by)], kept_in.at[by], kept_send.at[by], kept_recv.at[by], peer(by)
        )
        copy.start()
        sent.append(copy)

    forward = table_ref[0], table_ref[1]
    backward = table_ref[2], table_ref[3]
    column_block = lax.rem(lax.broadcasted_iota(jnp.int32, (1, 640), 1), 64) // 8

    @pl.loop(0, D // 256)
    def _(index):
        columns = pl.ds(pl.multiple_of(index * 256, 256), 256)
        moment = beta_decay * mom_ref[:, columns].astype(F32) + grad_ref[:, columns]
        halfway = split_dot(forward, halves(moment))
        coeffs = split_dot(halves(halfway), backward)
        sparse_rows = []
        for a in range(4):
            numbers = [own_ref[a, k : k + 1, columns] for k in range(4)]
            folded = [jnp.zeros((8, 256), F32)] * 4
            for r in range(8):
                piece = coeffs[64 * a + 8 * r : 64 * a + 8 * r + 8, :]
                here = column_block[:, :256] + 8 * r
                kept = jnp.zeros((8, 256), F32)
                for k in range(4):
                    one = jnp.where(numbers[k] == here, piece, 0.0)
                    folded[k] += one
                    kept += one
                sparse_rows.append(kept)
            picked[a, :, columns] = jnp.concatenate(folded, axis=0).astype(BF16)
        sparse = jnp.concatenate(sparse_rows, axis=0)
        halfway = split_dot(backward, halves(sparse))
        removed = split_dot(halves(halfway), forward)
        new_mom_ref[:, columns] = (moment - removed).astype(BF16)

    for c in range(4):
        for a in range(4):
            packed[a * 4 + c] = jnp.dot(
                picked[a, :, 640 * c : 640 * c + 640], fold_ref[...], preferred_element_type=F32
            ).astype(BF16)
    for by in range(1, REPS):
        copy = copy_to(
            packed.at[peer(by)], packed_in.at[by], pack_send.at[by], pack_recv.at[by], peer(by)
        )
        copy.start()
        sent.append(copy)
    packed_in[0] = packed[rep]
    kept_in[0] = kept_ref[rep]
    for by in range(1, REPS):
        copy_to(
            kept_in.at[by], kept_in.at[by], kept_send.at[by], kept_recv.at[by], peer(by)
        ).wait_recv()
        copy_to(
            packed_in.at[by], packed_in.at[by], pack_send.at[by], pack_recv.at[by], peer(by)
        ).wait_recv()
    sums = [jnp.zeros((8, 640), F32)] * 8
    for by in range(REPS):
        values = jnp.dot(packed_in[by], spread_ref[...], preferred_element_type=F32)
        for k in range(4):
            numbers = kept_in[by, k : k + 1, :]
            for r in range(8):
                sums[r] += jnp.where(
                    numbers == column_block + 8 * r, values[8 * k : 8 * k + 8, :], 0.0
                )
    summed = jnp.concatenate(sums, axis=0)
    halfway = split_dot((table_ref[2, :64, :64], table_ref[3, :64, :64]), halves(summed))
    a, c = rep // 4, lax.rem(rep, 4)
    mine = weight_ref[
        pl.ds(pl.multiple_of(a * 64, 64), 64), pl.ds(pl.multiple_of(c * 640, 128), 640)
    ].astype(F32)
    for part in range(5):
        columns = slice(128 * part, 128 * part + 128)
        update = split_dot(
            halves(halfway[:, columns]), (table_ref[0, :128, :128], table_ref[1, :128, :128])
        )
        tile[:, columns] = (mine[:, columns] - (step_rate / REPS) * update).astype(BF16)

    def place(owner):
        return new_weight_ref.at[
            pl.ds(pl.multiple_of(owner // 4 * 64, 64), 64),
            pl.ds(pl.multiple_of(lax.rem(owner, 4) * 640, 128), 640),
        ]

    chip, core = rep // 2, lax.rem(rep, 2)
    twin = chip * 2 + 1 - core
    for by in range(0, 8):
        target = twin if by == 0 else lax.rem(chip + by, 8) * 2 + core
        copy = copy_to(tile, place(rep), tile_send.at[by], tile_recv.at[by], target)
        copy.start()
        sent.append(copy)
    own = place(rep)
    own[...] = tile[...]
    for by in range(1, 8):
        owner = lax.rem(chip + 8 - by, 8) * 2 + core
        copy_to(tile, place(owner), tile_send.at[by], tile_recv.at[by], twin).wait_recv()
        copy = copy_to(
            place(owner), place(owner), tile_send.at[by + 8], tile_recv.at[by + 8], twin
        )
        copy.start()
        sent.append(copy)
    copy_to(tile, place(twin), tile_send.at[0], tile_recv.at[0], twin).wait_recv()
    for by in range(1, 8):
        owner = lax.rem(chip + 8 - by, 8) * 2 + 1 - core
        copy_to(
            place(owner), place(owner), tile_send.at[by + 8], tile_recv.at[by + 8], twin
        ).wait_recv()
    for copy in sent:
        copy.wait_send()


def tables():
    n = np.arange(64, dtype=np.float64)
    scale = np.where(n == 0, np.sqrt(1.0 / 64.0), np.sqrt(2.0 / 64.0))
    cosine = scale[:, None] * np.cos(np.pi * (2.0 * n[None, :] + 1.0) * n[:, None] / 128.0)
    block = np.kron(np.eye(4), cosine).astype(np.float32)
    parts = []
    for matrix in (block, block.T):
        high = matrix.astype(BF16)
        parts += [high, (matrix - high.astype(np.float32)).astype(BF16)]
    column = np.arange(640)
    fold = np.zeros((640, 128), np.float32)
    fold[column, column // 64 * 8 + column % 8] = 1.0
    return np.stack(parts), fold.astype(BF16), np.ascontiguousarray(fold.T).astype(BF16)


def shards(tokens, out_grads, weight, momentum, kept_blocks):
    table, fold, spread = tables()
    gradient = reduced_gradient(out_grads, tokens)
    numbers = jnp.repeat(kept_blocks[0].transpose(0, 2, 1), 64, axis=2)
    numbers = jnp.pad(numbers, ((0, 0), (0, 4), (0, 0)))
    by_peer = numbers.reshape(4, 8, 4, 640).transpose(0, 2, 1, 3).reshape(16, 8, 640)
    return codec(gradient, momentum[0], numbers, by_peer, weight, table, fold, spread)


def codec(gradient, momentum, numbers, by_peer, weight, table, fold, spread):
    vmem = pl.BlockSpec(memory_space=pltpu.VMEM)
    dma = pltpu.SemaphoreType.DMA((REPS,))

    new_weight, new_momentum = pl.pallas_call(
        codec_kernel,
        out_shape=(
            jax.ShapeDtypeStruct((ROWS, D), BF16),
            jax.ShapeDtypeStruct((ROWS, D), BF16),
        ),
        in_specs=[vmem] * 8,
        out_specs=(vmem, vmem),
        scratch_shapes=[
            pltpu.VMEM((4, 32, D), BF16),
            pltpu.VMEM((REPS, 32, 128), BF16),
            pltpu.VMEM((REPS, 32, 128), BF16),
            pltpu.VMEM((REPS, 8, 640), jnp.int32),
            pltpu.VMEM((64, 640), BF16),
            dma, dma, dma, dma, dma, dma,
        ],
        compiler_params=pltpu.CompilerParams(
            collective_id=1, has_side_effects=True, vmem_limit_bytes=40 * 2**20
        ),
    )(gradient, momentum, numbers, by_peer, weight, table, fold, spread)
    return new_weight, new_momentum[None]


def solution(mesh):
    placed = (
        P(("rep", "fsdp"), None),
        P(("rep", "fsdp"), None),
        P("fsdp", None),
        P("rep", "fsdp", None),
        P("rep", "fsdp", None, None),
    )
    return jax.shard_map(
        shards,
        mesh=mesh,
        in_specs=placed,
        out_specs=(P("fsdp", None), P("rep", "fsdp", None)),
        check_vma=False,
    )
```

time: 459 us -> 220 us (0.48); the launches traced: 453 us -> 220 us
  waiting for transfers between devices: 253 us -> 0 us
  Pallas kernels: 0 us -> 214 us
  local copies, waits for them, and re-layouts: 81.9 us -> 4.92 us
  matrix products: 75.1 us -> 0 us
  blocking collectives: 19.1 us -> 0 us
  between operations: 14.4 us -> 0.77 us
  other arithmetic: 9.55 us -> 0.02 us
    reduce_scatter x1 -> x0, waiting for transfers between devices: 253 us -> none  [shards(): lax.psum_scatter(lax.dot_general(out_grads, tokens, (((0,), (0,)), ((), (...]
    pallas_call x0 -> x2, Pallas kernels: none -> 214 us  [the longest x1 174 us: reduced_gradient(): pl.pallas_call(scatter_kernel, out_shape=jax.ShapeDtypeStruct((ROWS, D),...]
    dot_general x10 -> x0, matrix products: 75.1 us -> none  [the longest x1 17.7 us: shards(): lax.dot_general(out_grads, tokens, (((0,), (0,)), ((), ())), preferred_el...]
    transpose x8 -> x0, local copies, waits for them, and re-layouts: 31.3 us -> none  [the longest x1 7.3 us: shards(): jnp.einsum('rbkc,rkwc->bwc', masks, peer_picked, precision=lax.Precision....]
    reshape x7 -> x1, local copies, waits for them, and re-layouts: 28 us -> 0.15 us  [shards(): numbers = jnp.repeat(kept_blocks[0].transpose(0, 2, 1), 64, axis=2)]
    all_gather x1 -> x0, blocking collectives: 19.1 us -> none  [shards(): peer_chosen = lax.all_gather(chosen[None], 'rep', axis=0, tiled=True)]
    mul x3 -> x0, local copies, waits for them, and re-layouts: 16.2 us -> none  [shards(): step_rate * update]
  transfers between devices with their start and end apart: 2 -> 0, of which waited for: 1 -> 0; matrix products, arithmetic and copies ran while one was open for 11% -> 0% of each run, Pallas kernels for 0% -> 0%
where the time goes in v1:
time: 220 us
  Pallas kernels  214 us (97%)
  local copies, waits for them, and re-layouts  4.92 us (2%)
    pallas_call x1, Pallas kernels, reduced_gradient(): pl.pallas_call(scatter_kernel, out_shape=jax.ShapeDtypeStruct((ROWS, D),...  174 us
    pallas_call x1, Pallas kernels, codec(): pl.pallas_call(codec_kernel, out_shape=(jax.ShapeDtypeStruct((ROWS, D), B...  39.5 us

profile of v1, /device:TPU:1, one launch (start us, length us, event | category | flops | bytes accessed | tf_op | source)
XLA Modules:
  0.0 219.6 jit_solution(5124894940026878444)
XLA Ops:
  0.6 0.8 broadcast_in_dim.6
  1.5 0.1 reshape.11
  1.7 0.0 copy-start.1
  1.7 0.0 copy-start.2
  1.8 0.0 copy-start.3
  1.8 0.0 copy-start.4
  1.8 0.0 copy-start.5
  1.8 174.4 %shard_map.95.grad_ref = f32[256,2560]{1,0:T(8,128)} custom-call(bf16[512,4096]{1,0:T(8,128)(2,1)} %g_hbm.1, bf16[512,2560]{1,0:T(8,128)(2,1)} %t_ref.1), custom_call_target="tpu_custom_call" | custom-call | flops 10737418240 | bytes 6815744 | tf_op jit(solution)/shard_map/pallas_call | solution.py:185
  176.2 0.0 copy-done.1
  176.2 0.0 copy-done.2
  176.2 0.0 copy-done.3
  176.2 0.0 copy-done.4
  176.2 0.0 copy-done.5
  176.2 0.0 copy-start
  176.2 1.7 copy-done
  178.0 39.5 %shard_map.96 = (bf16[256,2560]{1,0:T(8,128)(2,1)S(1)}, bf16[256,2560]{1,0:T(8,128)(2,1)S(1)}) custom-call(f32[256,2560]{1,0:T(8,128)S(1)} %copy-done, bf16[256,2560]{1,0:T(8,128)(2,1)S(1)} %bitcast.9, s32[4,8,2560]{2,1,0:T(8,128)S(1)} %pad.4.own_ref, s32[16,8,640]{2,1,0:T(8,128)S(1)} %bitcast.8, bf16[256,2560]{1,0:T(8,128)(2,1)S(1)} %copy-done.2, ...), custom_call_target="tpu_custom_call" | custom-call | tf_op jit(solution)/shard_map/pallas_call | solution.py:382
  217.5 1.1 copy.12
  218.5 1.1 copy.13
  (3 shorter events, 0.1 us)
Async XLA Ops:
  1.7 174.4 %copy-start.1 = (bf16[1,256,2560]{2,1,0:T(8,128)(2,1)S(1)}, bf16[1,256,2560]{2,1,0:T(8,128)(2,1)}, u32[]{:S(2)}) copy-start(bf16[1,256,2560]{2,1,0:T(8,128)(2,1)} %param.11) | copy-start | bytes 3932164
  1.7 174.4 %copy-start.2 = (bf16[256,2560]{1,0:T(8,128)(2,1)S(1)}, bf16[256,2560]{1,0:T(8,128)(2,1)}, u32[]{:S(2)}) copy-start(bf16[256,2560]{1,0:T(8,128)(2,1)} %weight_ref.1) | copy-start | bytes 3932164
  1.8 174.4 %copy-start.3 = (bf16[4,256,256]{2,1,0:T(8,128)(2,1)S(1)}, bf16[4,256,256]{2,1,0:T(8,128)(2,1)}, u32[]{:S(2)}) copy-start(bf16[4,256,256]{2,1,0:T(8,128)(2,1)} %constant.8.clone.table_ref) | copy-start | bytes 1572868
  1.8 174.4 %copy-start.4 = (bf16[128,640]{1,0:T(8,128)(2,1)S(1)}, bf16[128,640]{1,0:T(8,128)(2,1)}, u32[]{:S(2)}) copy-start(bf16[128,640]{1,0:T(8,128)(2,1)} %constant.10.clone.spread_ref) | copy-start | bytes 491524
  1.8 174.4 %copy-start.5 = (bf16[640,128]{1,0:T(8,128)(2,1)S(1)}, bf16[640,128]{1,0:T(8,128)(2,1)}, u32[]{:S(2)}) copy-start(bf16[640,128]{1,0:T(8,128)(2,1)} %constant.9.clone.fold_ref) | copy-start | bytes 491524
  176.2 1.7 copy-start

commit v2 on v0

v2 whole, which is shorter than its diff:
```python
import functools

import jax
import jax.numpy as jnp
import numpy as np
from jax import lax
from jax.experimental import pallas as pl
from jax.experimental.pallas import tpu as pltpu
from jax.sharding import PartitionSpec as P

beta_decay = 0.9
step_rate = 0.5

MESH = pl.DeviceIdType.MESH
F32 = jnp.float32
BF16 = jnp.bfloat16

D = 2560
ROWS = 256
SIDE = 4
REPS = 16

JOBS = (
    ("y", 0, 256),
    ("y", 512, 256),
    ("y", 1024, 256),
    ("y", 2048, 128),
    ("y", 2304, 128),
    ("z", 1536, 128),
    ("z", 1792, 128),
)
BATCHES = ((0, 512), (2048, 128))
ORDER = (
    ("far", 0), ("near", 0), ("near", 6), ("far", 1), ("far", 6), ("merge", 0), ("far", 5),
    ("merge", 6), ("near", 1), ("merge", 1), ("merge", 5), ("turn", 0), ("turn", 6), ("far", 2),
    ("relay", 0), ("near", 2), ("turn", 1), ("relay", 6), ("finish", 0), ("far", 3),
    ("relay", 1), ("merge", 2), ("near", 5), ("finish", 1), ("far", 4), ("finish", 6),
    ("near", 3), ("merge", 3), ("turn", 5), ("turn", 2), ("near", 4), ("merge", 4), ("relay", 2),
    ("turn", 3), ("relay", 5), ("finish", 2), ("relay", 3), ("finish", 3), ("turn", 4),
    ("finish", 5), ("pack", 0), ("relay", 4), ("decode", 0), ("finish", 4), ("pack", 1),
    ("spread", 0), ("decode", 1), ("spread", 1), ("gather", 0), ("gather", 1),
)


def split_dot(left, right):
    total = jnp.dot(left[0], right[0], preferred_element_type=F32)
    total += jnp.dot(left[0], right[1], preferred_element_type=F32)
    return total + jnp.dot(left[1], right[0], preferred_element_type=F32)


def halves(value):
    high = value.astype(BF16)
    return high, (value - high.astype(F32)).astype(BF16)


def iota(shape, axis):
    return lax.broadcasted_iota(jnp.int32, shape, axis)


def one_hot(where):
    return jnp.where(where, 1.0, 0.0).astype(BF16)


def step_kernel(
    g_hbm, t_hbm, mom_hbm, weight_hbm, table_hbm, own_ref, kept_ref,
    new_weight_ref, new_mom_ref,
    gt, stage, tokens, mom, grad, table, weight0, weight1,
    picked, packed, packed_in, kept_in, tile0, tile1, values, numbers_in,
    load_sem, send_sem, recv_sem, kept_send, kept_recv, pack_send, pack_recv,
    tile_send, tile_recv, *bufs,
):
    wide, thin = bufs[: len(JOBS)], bufs[len(JOBS) :]
    rep = lax.axis_index("rep")
    member = lax.axis_index("fsdp")
    pos = {"y": member // SIDE, "z": member % SIDE}
    chip, core = rep // 2, rep % 2
    place_x, place_z = chip // 2, chip % 2
    twin = chip * 2 + 1 - core

    def device(axis, index):
        if axis == "y":
            return (rep, index * SIDE + pos["z"])
        return (rep, pos["y"] * SIDE + index)

    def turn(index, by):
        return lax.rem(index + (by + SIDE), SIDE)

    def peer(by):
        return lax.rem(rep + by, REPS)

    row_tile, column_tile = rep // 4, rep % 4

    def tile_of(ref, batch, owner):
        first, width = BATCHES[batch]
        return ref.at[
            pl.ds(pl.multiple_of(owner // 4 * 64, 64), 64),
            pl.ds(pl.multiple_of(first + lax.rem(owner, 4) * width, 128), width),
        ]

    loads = {}

    def load(name, number, src, dst):
        loads[name] = pltpu.make_async_copy(src, dst, load_sem.at[number])
        loads[name].start()

    def load_group(block):
        group = turn(pos["y"], (2, 1, 3, 0)[block])
        columns = pl.ds(pl.multiple_of(group * 1024, 1024), 1024)
        load(block, block, g_hbm.at[:, columns], stage.at[block])

    load_group(0)
    load("t0", 4, t_hbm.at[:, :512], tokens.at[:, :512])
    for block in range(1, SIDE):
        load_group(block)
    load("t1", 5, t_hbm.at[:, 512:], tokens.at[:, 512:])
    load("mom", 6, mom_hbm, mom)
    load("table", 7, table_hbm, table)
    load("w0", 8, tile_of(weight_hbm, 0, rep), weight0)
    load("w1", 9, tile_of(weight_hbm, 1, rep), weight1)

    barrier = pltpu.get_barrier_semaphore()
    for axis in ("y", "z"):
        for by in (1, -1):
            pl.semaphore_signal(
                barrier, inc=1, device_id=device(axis, turn(pos[axis], by)), device_id_type=MESH
            )
    for by in range(1, REPS):
        pl.semaphore_signal(barrier, inc=1, device_id=(peer(by), member), device_id_type=MESH)

    def transpose(block):
        group = turn(pos["y"], (2, 1, 3, 0)[block])
        loads[block].wait()

        for part in range(SIDE):
            start = pl.multiple_of(group * 1024 + part * ROWS, ROWS)
            gt[pl.ds(start, ROWS), :] = stage[block, :, part * ROWS : part * ROWS + ROWS].T

    def partial(axis, group, other, column, width):
        owner = group * SIDE + other if axis == "y" else other * SIDE + group
        rows = pl.ds(pl.multiple_of(owner * ROWS, ROWS), ROWS)
        return jnp.dot(
            gt[rows, :], tokens[:, column : column + width], preferred_element_type=F32
        )

    sent = []

    def transfer(src, dst, sems, index, target):
        return pltpu.make_async_remote_copy(
            src_ref=src,
            dst_ref=dst,
            send_sem=sems[0].at[index],
            recv_sem=sems[1].at[index],
            device_id=target,
            device_id_type=MESH,
        )

    def send(*args):
        copy = transfer(*args)
        copy.start()
        sent.append(copy)

    def arrived(dst, sems, index):
        transfer(dst, dst, sems, index, (twin, member)).wait_recv()

    ring = (send_sem, recv_sem)
    kept_sems, pack_sems = (kept_send, kept_recv), (pack_send, pack_recv)
    tile_sems = (tile_send, tile_recv)

    def stage_outward(job, slot):
        axis, first, width = JOBS[job]
        m = pos[axis]
        for side, d in ((0, -1), (1, 1)):
            column = first + side * width
            buf = wide[job].at[side]
            group, target = (turn(m, 2), turn(m, d)) if slot == 0 else (turn(m, -d),) * 2
            for other in range(SIDE):
                buf[slot, other] = partial(axis, group, other, column, width).astype(BF16)
            send(buf.at[slot], buf.at[slot + 2], ring, (job, side, slot), device(axis, target))

    def stage_merge(job):
        axis, first, width = JOBS[job]
        m = pos[axis]
        for side, d in ((0, -1), (1, 1)):
            column = first + side * width
            buf = wide[job].at[side]
            arrived(buf.at[2], ring, (job, side, 0))

            for other in range(SIDE):
                total = partial(axis, turn(m, d), other, column, width)
                buf[2, other] = (total + buf[2, other].astype(F32)).astype(BF16)
            send(buf.at[2], buf.at[4], ring, (job, side, 2), device(axis, turn(m, d)))

    def stage_turn(job):
        axis, first, width = JOBS[job]
        other_axis = "z" if axis == "y" else "y"
        m, n = pos[axis], pos[other_axis]
        for side, d in ((0, -1), (1, 1)):
            column = first + side * width
            buf, low = wide[job].at[side], thin[job].at[side]
            arrived(buf.at[3], ring, (job, side, 1))
            arrived(buf.at[4], ring, (job, side, 2))
            for slot, other in ((0, turn(n, 2)), (1, turn(n, -d)), (2, turn(n, d)), (3, n)):
                total = (
                    partial(axis, m, other, column, width)
                    + buf[3, other].astype(F32)
                    + buf[4, other].astype(F32)
                )
                if slot == 3:
                    grad[:, column : column + width] = total
                else:
                    low[slot] = total.astype(BF16)
                if slot < 2:
                    target = turn(n, d) if slot == 0 else turn(n, -d)
                    send(
                        low.at[slot], low.at[slot + 3], ring, (job, side, slot + 3),
                        device(other_axis, target),
                    )

    def stage_relay(job):
        axis = "z" if JOBS[job][0] == "y" else "y"
        for side, d in ((0, -1), (1, 1)):
            low = thin[job].at[side]
            arrived(low.at[3], ring, (job, side, 3))
            low[3] = (low[2].astype(F32) + low[3].astype(F32)).astype(BF16)
            send(low.at[3], low.at[5], ring, (job, side, 5), device(axis, turn(pos[axis], d)))

    def stage_finish(job):
        _, first, width = JOBS[job]
        for side in (0, 1):
            arrived(thin[job].at[side, 4], ring, (job, side, 4))
            arrived(thin[job].at[side, 5], ring, (job, side, 5))
        forward = table[0, :width, :width], table[1, :width, :width]
        backward = table[2, :width, :width], table[3, :width, :width]
        position = (iota((1, width), 1) % 64) // 8

        @pl.loop(0, 2)
        def _(side):
            start = pl.multiple_of(first + side * width, 128)
            columns = pl.ds(start, width)
            low = thin[job].at[side]
            gradient = grad[:, columns] + low[4].astype(F32) + low[5].astype(F32)
            moment = beta_decay * mom[:, columns].astype(F32) + gradient
            halfway = split_dot((table[0], table[1]), halves(moment))
            coeffs = split_dot(halves(halfway), backward)
            span = start // 64 + iota((128, width), 1) // 64
            numbers = jnp.dot(
                own_ref[...].astype(F32).astype(BF16),
                one_hot(iota((128, width), 0) == span),
                preferred_element_type=F32,
            ).astype(jnp.int32)
            sparse_rows = []
            for a in range(4):
                folded = [jnp.zeros((8, width), F32)] * 4
                for r in range(8):
                    piece = coeffs[64 * a + 8 * r : 64 * a + 8 * r + 8, :]
                    kept = jnp.zeros((8, width), F32)
                    for k in range(4):
                        chosen = numbers[8 * a + k : 8 * a + k + 1, :] == position + 8 * r
                        one = jnp.where(chosen, piece, 0.0)
                        folded[k] += one
                        kept += one
                    sparse_rows.append(kept)
                picked[a, :, columns] = jnp.concatenate(folded, axis=0).astype(BF16)
            sparse = jnp.concatenate(sparse_rows, axis=0)
            halfway = split_dot((table[2], table[3]), halves(sparse))
            removed = split_dot(halves(halfway), forward)
            new_mom_ref[:, columns] = (moment - removed).astype(BF16)

    def stage_pack(batch):
        first, width = BATCHES[batch]
        column = iota((width, 128), 0)
        fold = one_hot(iota((width, 128), 1) == column // 64 * 8 + column % 8)
        for c in range(4):
            for a in range(4):
                packed[batch, a * 4 + c] = jnp.dot(
                    picked[a, :, first + width * c : first + width * c + width],
                    fold,
                    preferred_element_type=F32,
                ).astype(BF16)
        for by in range(1, REPS):
            send(
                packed.at[batch, peer(by)], packed_in.at[batch, by], pack_sems, (batch, by),
                (peer(by), member),
            )
        packed_in[batch, 0] = packed[batch, rep]

    def stage_decode(batch):
        width = BATCHES[batch][1]
        column = iota((128, width), 1)
        lane = iota((128, width), 0)
        if batch == 0:
            kept_in[0] = kept_ref[rep]
            for by in range(1, REPS):
                arrived(kept_in.at[by], kept_sems, (by,))
        for by in range(1, REPS):
            arrived(packed_in.at[batch, by], pack_sems, (batch, by))
        values[:, :width] = jnp.dot(
            packed_in[batch].reshape(REPS * 32, 128),
            one_hot(lane == column // 64 * 8 + column % 8),
            preferred_element_type=F32,
        )
        numbers_in[:, :width] = jnp.dot(
            kept_in[...].reshape(REPS * 8, 128).astype(F32).astype(BF16),
            one_hot(lane == 8 * batch + column // 64),
            preferred_element_type=F32,
        ).astype(jnp.int32)
        position = (iota((1, width), 1) % 64) // 8

        def add(r, sums):
            sums = list(sums)
            value = values[pl.ds(pl.multiple_of(r * 32, 32), 32), :width]
            number = numbers_in[pl.ds(pl.multiple_of(r * 8, 8), 8), :width]
            for k in range(4):
                for b in range(8):
                    sums[b] += jnp.where(
                        number[k : k + 1, :] == position + 8 * b, value[8 * k : 8 * k + 8, :], 0.0
                    )
            return tuple(sums)

        sums = lax.fori_loop(0, REPS, add, (jnp.zeros((8, width), F32),) * 8)
        summed = jnp.concatenate(sums, axis=0)
        halfway = split_dot((table[2, :64, :64], table[3, :64, :64]), halves(summed))
        weight, tile = ((weight0, tile0), (weight1, tile1))[batch]
        loads["w%d" % batch].wait()
        for part in range(width // 128):
            columns = slice(128 * part, 128 * part + 128)
            update = split_dot(
                halves(halfway[:, columns]), (table[0, :128, :128], table[1, :128, :128])
            )
            fresh = weight[:, columns].astype(F32) - (step_rate / REPS) * update
            tile[:, columns] = fresh.astype(BF16)
        own = tile_of(new_weight_ref, batch, rep)
        send(tile, own, tile_sems, (batch, 0), (twin, member))
        if batch == 0:
            send(tile, own, tile_sems, (batch, 1), (rep + 2 - 4 * place_z, member))
            for by in range(1, 4):
                send(tile, own, tile_sems, (batch, 1 + by), (lax.rem(rep + 4 * by, REPS), member))
        else:
            for by in range(1, 8):
                target = lax.rem(chip + by, 8) * 2 + core
                send(tile, own, tile_sems, (batch, by), (target, member))
        own[...] = tile[...]

    def sources(batch, of_core):
        if batch == 1:
            return [(by, lax.rem(chip + 8 - by, 8) * 2 + of_core) for by in range(1, 8)]
        found = [(1, place_x * 4 + (1 - place_z) * 2 + of_core)]
        for shift, level in ((1, place_z), (4, 1 - place_z)):
            for by in range(1, 4):
                owner = lax.rem(place_x + 4 - by, 4) * 4 + level * 2 + of_core
                found.append((shift + by, owner))
        return found

    def stage_spread(batch):
        for number, owner in sources(batch, core):
            part = tile_of(new_weight_ref, batch, owner)
            arrived(part, tile_sems, (batch, number))
            send(part, part, tile_sems, (batch, number + 7), (twin, member))
            if batch == 0 and number == 1:
                for by in range(1, 4):
                    target = lax.rem(rep + 4 * by, REPS)
                    send(part, part, tile_sems, (batch, 4 + by), (target, member))

    def stage_gather(batch):
        arrived(tile_of(new_weight_ref, batch, twin), tile_sems, (batch, 0))
        for number, owner in sources(batch, 1 - core):
            part = tile_of(new_weight_ref, batch, owner)
            arrived(part, tile_sems, (batch, number + 7))

    ready = set()

    def prepare(name, which):
        if name in ("far", "near", "merge", "turn"):
            axis = JOBS[which][0]
            blocks = {"far": (0,), "near": (1, 2), "merge": (1, 2), "turn": (3,)}[name]
            needs = list(blocks if axis == "y" else range(SIDE)) + ["t0"]
            needs += ["t1"] if JOBS[which][1] >= 512 else []
        else:
            needs = ["mom", "table"] if name == "finish" else []
        for need in needs:
            if need not in ready:
                ready.add(need)
                if need in range(SIDE):
                    transpose(need)
                else:
                    loads[need].wait()

    stages = {
        "far": lambda job: stage_outward(job, 0), "near": lambda job: stage_outward(job, 1),
        "merge": stage_merge, "turn": stage_turn, "relay": stage_relay, "finish": stage_finish,
        "pack": stage_pack, "decode": stage_decode, "spread": stage_spread,
        "gather": stage_gather,
    }
    prepare(*ORDER[0])
    pl.semaphore_wait(barrier, 4 + REPS - 1)
    for number, (name, which) in enumerate(ORDER):
        if number == 4:
            for by in range(1, REPS):
                send(kept_ref.at[peer(by)], kept_in.at[by], kept_sems, (by,), (peer(by), member))
        prepare(name, which)
        stages[name](which)
    for copy in sent:
        copy.wait_send()


def tables():
    n = np.arange(64, dtype=np.float64)
    scale = np.where(n == 0, np.sqrt(1.0 / 64.0), np.sqrt(2.0 / 64.0))
    cosine = scale[:, None] * np.cos(np.pi * (2.0 * n[None, :] + 1.0) * n[:, None] / 128.0)
    block = np.kron(np.eye(4), cosine).astype(np.float32)
    parts = []
    for matrix in (block, block.T):
        high = matrix.astype(BF16)
        parts += [high, (matrix - high.astype(np.float32)).astype(BF16)]
    return np.stack(parts)


def shards(tokens, out_grads, weight, momentum, kept_blocks):
    numbers = kept_blocks[0].transpose(0, 2, 1)
    own = jnp.pad(numbers, ((0, 0), (0, 4), (0, 88))).reshape(32, 128)
    peers = jnp.concatenate(
        [numbers[:, :, :32].reshape(4, 4, 4, 8), numbers[:, :, 32:].reshape(4, 4, 4, 2)], axis=3
    )
    peers = jnp.pad(peers.transpose(0, 2, 1, 3), ((0, 0), (0, 0), (0, 4), (0, 118)))
    vmem = pl.BlockSpec(memory_space=pltpu.VMEM)
    hbm = pl.BlockSpec(memory_space=pl.ANY)
    dma = pltpu.SemaphoreType.DMA
    new_weight, new_momentum = pl.pallas_call(
        step_kernel,
        out_shape=(
            jax.ShapeDtypeStruct((ROWS, D), BF16),
            jax.ShapeDtypeStruct((ROWS, D), BF16),
        ),
        in_specs=[hbm] * 5 + [vmem] * 2,
        out_specs=(vmem, vmem),
        scratch_shapes=[
            pltpu.VMEM((4096, 512), BF16),
            pltpu.VMEM((SIDE, 512, 1024), BF16),
            pltpu.VMEM((512, D), BF16),
            pltpu.VMEM((ROWS, D), BF16),
            pltpu.VMEM((ROWS, D), F32),
            pltpu.VMEM((4, 256, 256), BF16),
            pltpu.VMEM((64, 512), BF16),
            pltpu.VMEM((64, 128), BF16),
            pltpu.VMEM((4, 32, D), BF16),
            pltpu.VMEM((2, REPS, 32, 128), BF16),
            pltpu.VMEM((2, REPS, 32, 128), BF16),
            pltpu.VMEM((REPS, 8, 128), jnp.int32),
            pltpu.VMEM((64, 512), BF16),
            pltpu.VMEM((64, 128), BF16),
            pltpu.VMEM((REPS * 32, 512), F32),
            pltpu.VMEM((REPS * 8, 512), jnp.int32),
            dma((10,)),
            dma((len(JOBS), 2, 6)),
            dma((len(JOBS), 2, 6)),
            dma((REPS,)),
            dma((REPS,)),
            dma((2, REPS)),
            dma((2, REPS)),
            dma((2, REPS)),
            dma((2, REPS)),
        ]
        + [pltpu.VMEM((2, 5, SIDE, ROWS, job[2]), BF16) for job in JOBS]
        + [pltpu.VMEM((2, 6, ROWS, job[2]), BF16) for job in JOBS],
        compiler_params=pltpu.CompilerParams(
            collective_id=0, has_side_effects=True, vmem_limit_bytes=62 * 2**20
        ),
        cost_estimate=pl.CostEstimate(
            flops=2 * 512 * 4096 * D, bytes_accessed=2 * 512 * (4096 + D), transcendentals=0
        ),
    )(out_grads, tokens, momentum[0], weight, tables(), own, peers.reshape(REPS, 8, 128))
    return new_weight, new_momentum[None]


def solution(mesh):
    placed = (
        P(("rep", "fsdp"), None),
        P(("rep", "fsdp"), None),
        P("fsdp", None),
        P("rep", "fsdp", None),
        P("rep", "fsdp", None, None),
    )
    return jax.shard_map(
        shards,
        mesh=mesh,
        in_specs=placed,
        out_specs=(P("fsdp", None), P("rep", "fsdp", None)),
        check_vma=False,
    )
```

time: 459 us -> 198 us (0.43); the launches traced: 453 us -> 198 us
  waiting for transfers between devices: 253 us -> 0 us
  Pallas kernels: 0 us -> 191 us
  local copies, waits for them, and re-layouts: 81.9 us -> 6.15 us
  matrix products: 75.1 us -> 0 us
  blocking collectives: 19.1 us -> 0 us
  between operations: 14.4 us -> 0.66 us
  other arithmetic: 9.55 us -> 0.09 us
    reduce_scatter x1 -> x0, waiting for transfers between devices: 253 us -> none  [shards(): lax.psum_scatter(lax.dot_general(out_grads, tokens, (((0,), (0,)), ((), (...]
    pallas_call x0 -> x1, Pallas kernels: none -> 191 us  [shards(): pl.pallas_call(step_kernel, out_shape=(jax.ShapeDtypeStruct((ROWS, D), BF...]
    dot_general x10 -> x0, matrix products: 75.1 us -> none  [the longest x1 17.7 us: shards(): lax.dot_general(out_grads, tokens, (((0,), (0,)), ((), ())), preferred_el...]
    transpose x8 -> x0, local copies, waits for them, and re-layouts: 31.3 us -> none  [the longest x1 7.3 us: shards(): jnp.einsum('rbkc,rkwc->bwc', masks, peer_picked, precision=lax.Precision....]
    reshape x7 -> x4, local copies, waits for them, and re-layouts: 28 us -> 1 us  [the longest x1 0.63 us: shards(): own = jnp.pad(numbers, ((0, 0), (0, 4), (0, 88))).reshape(32, 128)]
    all_gather x1 -> x0, blocking collectives: 19.1 us -> none  [shards(): peer_chosen = lax.all_gather(chosen[None], 'rep', axis=0, tiled=True)]
    mul x3 -> x0, local copies, waits for them, and re-layouts: 16.2 us -> none  [shards(): step_rate * update]
  transfers between devices with their start and end apart: 2 -> 0, of which waited for: 1 -> 0; matrix products, arithmetic and copies ran while one was open for 11% -> 0% of each run, Pallas kernels for 0% -> 0%
where the time goes in v2:
time: 198 us
  Pallas kernels  191 us (96%)
  local copies, waits for them, and re-layouts  6.15 us (3%)
    pallas_call x1, Pallas kernels, shards(): pl.pallas_call(step_kernel, out_shape=(jax.ShapeDtypeStruct((ROWS, D), BF...  191 us
    unnamed x6, local copies, waits for them, and re-layouts  4.5 us

profile of v2, /device:TPU:1, one launch (start us, length us, event | category | flops | bytes accessed | tf_op | source)
XLA Modules:
  0.0 198.1 jit_solution(17086414425208637486)
XLA Ops:
  0.6 0.8 copy.8
  1.4 0.1 copy.12
  1.5 0.6 pad_bitcast_fusion.own_ref
  2.2 0.2 copy.10
  2.3 0.2 copy.11
  2.5 0.1 add_bitcast_fusion
  2.6 0.6 pad.9
  3.3 191.2 %shard_map.77 = (bf16[256,2560]{1,0:T(8,128)(2,1)}, bf16[256,2560]{1,0:T(8,128)(2,1)}) custom-call(bf16[512,4096]{1,0:T(8,128)(2,1)} %g_hbm.1, bf16[512,2560]{1,0:T(8,128)(2,1)} %t_hbm.1, bf16[256,2560]{1,0:T(8,128)(2,1)} %bitcast.19, bf16[256,2560]{1,0:T(8,128)(2,1)} %weight_hbm.1, bf16[4,256,256]{2,1,0:T(8,128)(2,1)} %constant.4.clone.table_hbm, ...), custom_call_target="tpu_custom_call" | custom-call | flops 10737418240 | bytes 6815744 | tf_op jit(solution)/shard_map/pallas_call | solution.py:428
  194.5 0.0 copy-start
  194.5 2.6 %copy.15 = bf16[256,2560]{1,0:T(8,128)(2,1)} copy(bf16[256,2560]{1,0:T(8,128)(2,1)} %get-tuple-element.8) | data formatting | bytes 2621440
  197.0 0.0 copy-done
  197.0 1.1 copy.16
  (2 shorter events, 0.0 us)
Async XLA Ops:
  194.5 2.6 %copy-start = (bf16[256,2560]{1,0:T(8,128)(2,1)S(1)}, bf16[256,2560]{1,0:T(8,128)(2,1)}, u32[]{:S(2)}) copy-start(bf16[256,2560]{1,0:T(8,128)(2,1)} %get-tuple-element.5) | copy-start | bytes 3932164

commit v3 on v2

--- a/solution.py
+++ b/solution.py
@@ -21,25 +21,39 @@
 REPS = 16
 
 JOBS = (
-    ("y", 0, 256),
-    ("y", 512, 256),
-    ("y", 1024, 256),
-    ("y", 2048, 128),
-    ("y", 2304, 128),
-    ("z", 1536, 128),
-    ("z", 1792, 128),
+    ("h", 0, 256),
+    ("h", 256, 256),
+    ("e", 512, 256),
+    ("e", 768, 256),
+    ("e", 1024, 256),
+    ("e", 1280, 256),
+    ("z", 1536, 256),
+    ("e", 2048, 128),
+    ("e", 2176, 128),
+    ("e", 2304, 128),
+    ("e", 2432, 128),
 )
 BATCHES = ((0, 512), (2048, 128))
 ORDER = (
-    ("far", 0), ("near", 0), ("near", 6), ("far", 1), ("far", 6), ("merge", 0), ("far", 5),
-    ("merge", 6), ("near", 1), ("merge", 1), ("merge", 5), ("turn", 0), ("turn", 6), ("far", 2),
-    ("relay", 0), ("near", 2), ("turn", 1), ("relay", 6), ("finish", 0), ("far", 3),
-    ("relay", 1), ("merge", 2), ("near", 5), ("finish", 1), ("far", 4), ("finish", 6),
-    ("near", 3), ("merge", 3), ("turn", 5), ("turn", 2), ("near", 4), ("merge", 4), ("relay", 2),
-    ("turn", 3), ("relay", 5), ("finish", 2), ("relay", 3), ("finish", 3), ("turn", 4),
-    ("finish", 5), ("pack", 0), ("relay", 4), ("decode", 0), ("finish", 4), ("pack", 1),
-    ("spread", 0), ("decode", 1), ("spread", 1), ("gather", 0), ("gather", 1),
+    ("tokens", 4), ("tokens", 3), ("inputs", 0), ("half", 0), ("far", 6), ("tokens", 9),
+    ("half", 1), ("inputs", 1), ("near", 6), ("merge", 6), ("tokens", 2), ("quarter", 0),
+    ("exchange", 4), ("exchange", 3), ("exchange", 9), ("tokens", 5), ("tokens", 7),
+    ("quarter", 1), ("turn", 4), ("tokens", 8), ("tokens", 10), ("exchange", 2), ("turn", 6),
+    ("turn", 3), ("relay", 4), ("turn", 9), ("turn", 0), ("relay", 3), ("relay", 9),
+    ("exchange", 5), ("finish", 4), ("exchange", 7), ("turn", 2), ("relay", 0), ("finish", 3),
+    ("finish", 9), ("turn", 1), ("relay", 2), ("exchange", 8), ("exchange", 10), ("turn", 5),
+    ("finish", 0), ("relay", 6), ("relay", 1), ("turn", 7), ("relay", 5), ("turn", 8),
+    ("finish", 2), ("finish", 1), ("turn", 10), ("relay", 7), ("finish", 6), ("finish", 5),
+    ("relay", 8), ("pack", 0), ("relay", 10), ("decode", 0), ("finish", 8), ("finish", 7),
+    ("finish", 10), ("pack", 1), ("spread", 0), ("decode", 1), ("spread", 1), ("gather", 0),
+    ("gather", 1),
 )
+
+
+NEEDS = {
+    "half": (0, 1), "quarter": (2,), "exchange": (0,), "turn": (3,), "far": (), "near": (),
+    "merge": (),
+}
 
 
 def split_dot(left, right):
@@ -62,11 +76,11 @@
 
 
 def step_kernel(
-    g_hbm, t_hbm, mom_hbm, weight_hbm, table_hbm, own_ref, kept_ref,
+    g_hbm, t_hbm, mom_hbm, weight_hbm, table_hbm, kept_ref,
     new_weight_ref, new_mom_ref,
-    gt, stage, tokens, mom, grad, table, weight0, weight1,
+    gt, gp, stage, tokens, tp, own_ref, mom, grad, table, weight0, weight1,
     picked, packed, packed_in, kept_in, tile0, tile1, values, numbers_in,
-    load_sem, send_sem, recv_sem, kept_send, kept_recv, pack_send, pack_recv,
+    load_sem, send_sem, recv_sem, pair_send, pair_recv, kept_send, kept_recv, pack_send, pack_recv,
     tile_send, tile_recv, *bufs,
 ):
     wide, thin = bufs[: len(JOBS)], bufs[len(JOBS) :]
@@ -97,6 +111,10 @@
             pl.ds(pl.multiple_of(first + lax.rem(owner, 4) * width, 128), width),
         ]
 
+    mate = pos["y"] + 1 - 2 * (pos["y"] % 2)
+    other_mate = SIDE - 1 - pos["y"]
+    groups = (other_mate, SIDE - 1 - mate, mate, pos["y"])
+
     loads = {}
 
     def load(name, number, src, dst):
@@ -104,8 +122,7 @@
         loads[name].start()
 
     def load_group(block):
-        group = turn(pos["y"], (2, 1, 3, 0)[block])
-        columns = pl.ds(pl.multiple_of(group * 1024, 1024), 1024)
+        columns = pl.ds(pl.multiple_of(groups[block] * 1024, 1024), 1024)
         load(block, block, g_hbm.at[:, columns], stage.at[block])
 
     load_group(0)
@@ -128,7 +145,7 @@
         pl.semaphore_signal(barrier, inc=1, device_id=(peer(by), member), device_id_type=MESH)
 
     def transpose(block):
-        group = turn(pos["y"], (2, 1, 3, 0)[block])
+        group = groups[block]
         loads[block].wait()
 
         for part in range(SIDE):
@@ -141,6 +158,21 @@
         return jnp.dot(
             gt[rows, :], tokens[:, column : column + width], preferred_element_type=F32
         )
+
+    def received(number, other, column, width):
+        rows = pl.ds(pl.multiple_of(other * ROWS, ROWS), ROWS)
+        return jnp.dot(
+            gp[number, rows, :], tp[:, column : column + width], preferred_element_type=F32
+        )
+
+    def axes(job):
+        return ("z", "y") if JOBS[job][0] == "z" else ("y", "z")
+
+    def sides(job):
+        kind, first, width = JOBS[job]
+        if kind == "z":
+            return ((0, first, -1), (1, first + width, 1))
+        return ((0, first, -1 if job % 2 == 0 else 1),)
 
     sent = []
 
@@ -163,48 +195,94 @@
         transfer(dst, dst, sems, index, (twin, member)).wait_recv()
 
     ring = (send_sem, recv_sem)
+    pair_sems = (pair_send, pair_recv)
     kept_sems, pack_sems = (kept_send, kept_recv), (pack_send, pack_recv)
     tile_sems = (tile_send, tile_recv)
 
+    def stage_inputs(number):
+        start = pl.multiple_of(groups[1 + number] * 1024, 1024)
+        send(
+            gt.at[pl.ds(start, 1024), :], gp.at[number], pair_sems, (number,), device("y", mate)
+        )
+
+    def stage_tokens(job):
+        _, first, width = JOBS[job]
+        columns = slice(first, first + width)
+        send(tokens.at[:, columns], tp.at[:, columns], pair_sems, (2 + job,), device("y", mate))
+
+    def stage_half(job):
+        _, first, width = JOBS[job]
+        buf = wide[job]
+        for slot in (0, 1):
+            for other in range(SIDE):
+                buf[slot, other] = partial("y", groups[slot], other, first, width).astype(BF16)
+        send(buf.at[0:2], buf.at[2:4], ring, (job, 0, 0), device("y", other_mate))
+
+    def stage_quarter(job):
+        _, first, width = JOBS[job]
+        buf = wide[job]
+        arrived(buf.at[2:4], ring, (job, 0, 0))
+        for other in range(SIDE):
+            total = partial("y", mate, other, first, width)
+            buf[3, other] = (total + buf[3, other].astype(F32)).astype(BF16)
+        send(buf.at[3], buf.at[4], ring, (job, 0, 1), device("y", mate))
+
+    def stage_exchange(job):
+        _, first, width = JOBS[job]
+        buf = wide[job]
+        columns = slice(first, first + width)
+        arrived(tp.at[:, columns], pair_sems, (2 + job,))
+        for other in range(SIDE):
+            total = partial("y", other_mate, other, first, width)
+            buf[0, other] = (total + received(0, other, first, width)).astype(BF16)
+        send(buf.at[0], buf.at[1], ring, (job, 0, 0), device("y", other_mate))
+
     def stage_outward(job, slot):
-        axis, first, width = JOBS[job]
-        m = pos[axis]
-        for side, d in ((0, -1), (1, 1)):
-            column = first + side * width
+        width = JOBS[job][2]
+        m = pos["z"]
+        for side, column, d in sides(job):
             buf = wide[job].at[side]
             group, target = (turn(m, 2), turn(m, d)) if slot == 0 else (turn(m, -d),) * 2
             for other in range(SIDE):
-                buf[slot, other] = partial(axis, group, other, column, width).astype(BF16)
-            send(buf.at[slot], buf.at[slot + 2], ring, (job, side, slot), device(axis, target))
+                buf[slot, other] = partial("z", group, other, column, width).astype(BF16)
+            send(buf.at[slot], buf.at[slot + 2], ring, (job, side, slot), device("z", target))
 
     def stage_merge(job):
-        axis, first, width = JOBS[job]
-        m = pos[axis]
-        for side, d in ((0, -1), (1, 1)):
-            column = first + side * width
+        width = JOBS[job][2]
+        m = pos["z"]
+        for side, column, d in sides(job):
             buf = wide[job].at[side]
             arrived(buf.at[2], ring, (job, side, 0))
-
             for other in range(SIDE):
-                total = partial(axis, turn(m, d), other, column, width)
+                total = partial("z", turn(m, d), other, column, width)
                 buf[2, other] = (total + buf[2, other].astype(F32)).astype(BF16)
-            send(buf.at[2], buf.at[4], ring, (job, side, 2), device(axis, turn(m, d)))
+            send(buf.at[2], buf.at[4], ring, (job, side, 2), device("z", turn(m, d)))
 
     def stage_turn(job):
-        axis, first, width = JOBS[job]
-        other_axis = "z" if axis == "y" else "y"
+        kind, _, width = JOBS[job]
+        axis, other_axis = axes(job)
         m, n = pos[axis], pos[other_axis]
-        for side, d in ((0, -1), (1, 1)):
-            column = first + side * width
-            buf, low = wide[job].at[side], thin[job].at[side]
-            arrived(buf.at[3], ring, (job, side, 1))
-            arrived(buf.at[4], ring, (job, side, 2))
+        for side, column, d in sides(job):
+            low = thin[job].at[side]
+            if kind == "z":
+                buf = wide[job].at[side]
+                arrived(buf.at[3], ring, (job, side, 1))
+                arrived(buf.at[4], ring, (job, side, 2))
+                terms = (3, 4)
+            elif kind == "h":
+                buf = wide[job]
+                arrived(buf.at[4], ring, (job, side, 1))
+                terms = (2, 4)
+            else:
+                buf = wide[job]
+                arrived(buf.at[1], ring, (job, side, 0))
+                terms = (1,)
             for slot, other in ((0, turn(n, 2)), (1, turn(n, -d)), (2, turn(n, d)), (3, n)):
-                total = (
-                    partial(axis, m, other, column, width)
-                    + buf[3, other].astype(F32)
-                    + buf[4, other].astype(F32)
-                )
+                total = partial(axis, m, other, column, width)
+                if kind == "e":
+                    total += received(1, other, column, width)
+                for term in terms:
+                    total += buf[term, other].astype(F32)
                 if slot == 3:
                     grad[:, column : column + width] = total
                 else:
@@ -217,27 +295,23 @@
                     )
 
     def stage_relay(job):
-        axis = "z" if JOBS[job][0] == "y" else "y"
-        for side, d in ((0, -1), (1, 1)):
+        axis = axes(job)[1]
+        for side, column, d in sides(job):
             low = thin[job].at[side]
             arrived(low.at[3], ring, (job, side, 3))
             low[3] = (low[2].astype(F32) + low[3].astype(F32)).astype(BF16)
             send(low.at[3], low.at[5], ring, (job, side, 5), device(axis, turn(pos[axis], d)))
 
     def stage_finish(job):
-        _, first, width = JOBS[job]
-        for side in (0, 1):
-            arrived(thin[job].at[side, 4], ring, (job, side, 4))
-            arrived(thin[job].at[side, 5], ring, (job, side, 5))
+        width = JOBS[job][2]
+        backward = table[2, :width, :width], table[3, :width, :width]
         forward = table[0, :width, :width], table[1, :width, :width]
-        backward = table[2, :width, :width], table[3, :width, :width]
         position = (iota((1, width), 1) % 64) // 8
-
-        @pl.loop(0, 2)
-        def _(side):
-            start = pl.multiple_of(first + side * width, 128)
-            columns = pl.ds(start, width)
+        for side, start, _ in sides(job):
             low = thin[job].at[side]
+            arrived(low.at[4], ring, (job, side, 4))
+            arrived(low.at[5], ring, (job, side, 5))
+            columns = slice(start, start + width)
             gradient = grad[:, columns] + low[4].astype(F32) + low[5].astype(F32)
             moment = beta_decay * mom[:, columns].astype(F32) + gradient
             halfway = split_dot((table[0], table[1]), halves(moment))
@@ -285,11 +359,11 @@
         packed_in[batch, 0] = packed[batch, rep]
 
     def stage_decode(batch):
-        width = BATCHES[batch][1]
+        first, width = BATCHES[batch]
         column = iota((128, width), 1)
         lane = iota((128, width), 0)
         if batch == 0:
-            kept_in[0] = kept_ref[rep]
+            kept_in[0] = own_ref[pl.ds(pl.multiple_of(row_tile * 8, 8), 8), :]
             for by in range(1, REPS):
                 arrived(kept_in.at[by], kept_sems, (by,))
         for by in range(1, REPS):
@@ -301,7 +375,7 @@
         )
         numbers_in[:, :width] = jnp.dot(
             kept_in[...].reshape(REPS * 8, 128).astype(F32).astype(BF16),
-            one_hot(lane == 8 * batch + column // 64),
+            one_hot(lane == (first + column_tile * width) // 64 + column // 64),
             preferred_element_type=F32,
         ).astype(jnp.int32)
         position = (iota((1, width), 1) % 64) // 8
@@ -370,33 +444,48 @@
     ready = set()
 
     def prepare(name, which):
-        if name in ("far", "near", "merge", "turn"):
-            axis = JOBS[which][0]
-            blocks = {"far": (0,), "near": (1, 2), "merge": (1, 2), "turn": (3,)}[name]
-            needs = list(blocks if axis == "y" else range(SIDE)) + ["t0"]
-            needs += ["t1"] if JOBS[which][1] >= 512 else []
-        else:
-            needs = ["mom", "table"] if name == "finish" else []
+        needs = []
+        if name in NEEDS:
+            needs = list(range(SIDE) if JOBS[which][0] == "z" else NEEDS[name])
+            needs += ["t1" if JOBS[which][1] >= 512 else "t0"]
+            if JOBS[which][0] == "e":
+                needs += {"exchange": ["g0"], "turn": ["g1"]}[name]
+        elif name == "inputs":
+            needs = [1 + which]
+        elif name == "tokens":
+            needs = ["t1"]
+        elif name == "finish":
+            needs = ["mom", "table"]
         for need in needs:
-            if need not in ready:
-                ready.add(need)
-                if need in range(SIDE):
-                    transpose(need)
-                else:
-                    loads[need].wait()
+            if need in ready:
+                continue
+            ready.add(need)
+            if need in range(SIDE):
+                transpose(need)
+            elif need in ("g0", "g1"):
+                number = int(need[1])
+                arrived(gp.at[number], pair_sems, (number,))
+            else:
+                loads[need].wait()
 
     stages = {
+        "inputs": stage_inputs, "tokens": stage_tokens, "half": stage_half,
+        "quarter": stage_quarter, "exchange": stage_exchange,
         "far": lambda job: stage_outward(job, 0), "near": lambda job: stage_outward(job, 1),
         "merge": stage_merge, "turn": stage_turn, "relay": stage_relay, "finish": stage_finish,
         "pack": stage_pack, "decode": stage_decode, "spread": stage_spread,
         "gather": stage_gather,
     }
-    prepare(*ORDER[0])
+    own_ref[...] = jnp.zeros_like(own_ref)
+    for a in range(4):
+        own_ref[8 * a : 8 * a + 4, :40] = kept_ref[a]
+    prepare("inputs", 0)
     pl.semaphore_wait(barrier, 4 + REPS - 1)
     for number, (name, which) in enumerate(ORDER):
-        if number == 4:
+        if number == 8:
             for by in range(1, REPS):
-                send(kept_ref.at[peer(by)], kept_in.at[by], kept_sems, (by,), (peer(by), member))
+                rows = pl.ds(pl.multiple_of(peer(by) // 4 * 8, 8), 8)
+                send(own_ref.at[rows, :], kept_in.at[by], kept_sems, (by,), (peer(by), member))
         prepare(name, which)
         stages[name](which)
     for copy in sent:
@@ -417,11 +506,6 @@
 
 def shards(tokens, out_grads, weight, momentum, kept_blocks):
     numbers = kept_blocks[0].transpose(0, 2, 1)
-    own = jnp.pad(numbers, ((0, 0), (0, 4), (0, 88))).reshape(32, 128)
-    peers = jnp.concatenate(
-        [numbers[:, :, :32].reshape(4, 4, 4, 8), numbers[:, :, 32:].reshape(4, 4, 4, 2)], axis=3
-    )
-    peers = jnp.pad(peers.transpose(0, 2, 1, 3), ((0, 0), (0, 0), (0, 4), (0, 118)))
     vmem = pl.BlockSpec(memory_space=pltpu.VMEM)
     hbm = pl.BlockSpec(memory_space=pl.ANY)
     dma = pltpu.SemaphoreType.DMA
@@ -431,12 +515,15 @@
             jax.ShapeDtypeStruct((ROWS, D), BF16),
             jax.ShapeDtypeStruct((ROWS, D), BF16),
         ),
-        in_specs=[hbm] * 5 + [vmem] * 2,
+        in_specs=[hbm] * 5 + [vmem],
         out_specs=(vmem, vmem),
         scratch_shapes=[
             pltpu.VMEM((4096, 512), BF16),
+            pltpu.VMEM((2, 1024, 512), BF16),
             pltpu.VMEM((SIDE, 512, 1024), BF16),
             pltpu.VMEM((512, D), BF16),
+            pltpu.VMEM((512, D), BF16),
+            pltpu.VMEM((32, 128), jnp.int32),
             pltpu.VMEM((ROWS, D), BF16),
             pltpu.VMEM((ROWS, D), F32),
             pltpu.VMEM((4, 256, 256), BF16),
@@ -453,6 +540,8 @@
             dma((10,)),
             dma((len(JOBS), 2, 6)),
             dma((len(JOBS), 2, 6)),
+            dma((2 + len(JOBS),)),
+            dma((2 + len(JOBS),)),
             dma((REPS,)),
             dma((REPS,)),
             dma((2, REPS)),
@@ -460,15 +549,18 @@
             dma((2, REPS)),
             dma((2, REPS)),
         ]
-        + [pltpu.VMEM((2, 5, SIDE, ROWS, job[2]), BF16) for job in JOBS]
-        + [pltpu.VMEM((2, 6, ROWS, job[2]), BF16) for job in JOBS],
+        + [
+            pltpu.VMEM({"h": (5,), "e": (2,), "z": (2, 5)}[kind] + (SIDE, ROWS, width), BF16)
+            for kind, _, width in JOBS
+        ]
+        + [pltpu.VMEM((2 if kind == "z" else 1, 6, ROWS, width), BF16) for kind, _, width in JOBS],
         compiler_params=pltpu.CompilerParams(
-            collective_id=0, has_side_effects=True, vmem_limit_bytes=62 * 2**20
+            collective_id=0, has_side_effects=True, vmem_limit_bytes=52 * 2**20
         ),
         cost_estimate=pl.CostEstimate(
             flops=2 * 512 * 4096 * D, bytes_accessed=2 * 512 * (4096 + D), transcendentals=0
         ),
-    )(out_grads, tokens, momentum[0], weight, tables(), own, peers.reshape(REPS, 8, 128))
+    )(out_grads, tokens, momentum[0], weight, tables(), numbers)
     return new_weight, new_momentum[None]
 
 

time: 198 us -> 183 us (0.924)
  Pallas kernels: 191 us -> 177 us
    pallas_call x1, Pallas kernels: 191 us -> 177 us  [shards(): pl.pallas_call(step_kernel, out_shape=(jax.ShapeDtypeStruct((ROWS, D), BF...]
    unnamed x6 -> x8, local copies, waits for them, and re-layouts: 4.5 us -> 4.57 us
where the time goes in v3:
time: 183 us; the launch traced here: 182 us
  Pallas kernels  177 us (97%)
  local copies, waits for them, and re-layouts  4.57 us (2%)
    pallas_call x1, Pallas kernels, shards(): pl.pallas_call(step_kernel, out_shape=(jax.ShapeDtypeStruct((ROWS, D), BF...  177 us
    unnamed x8, local copies, waits for them, and re-layouts  4.57 us

profile of v3, /device:TPU:1, one launch (start us, length us, event | category | flops | bytes accessed | tf_op | source)
XLA Modules:
  0.0 182.4 jit_solution(16937597548006710104)
XLA Ops:
  0.6 0.0 copy-start
  0.6 0.7 copy-done
  1.3 0.0 copy-start.1
  1.3 1.0 copy-done.1
  2.4 177.2 %shard_map.77 = (bf16[256,2560]{1,0:T(8,128)(2,1)S(1)}, bf16[256,2560]{1,0:T(8,128)(2,1)}) custom-call(bf16[512,4096]{1,0:T(8,128)(2,1)} %g_hbm.1, bf16[512,2560]{1,0:T(8,128)(2,1)} %t_hbm.1, bf16[256,2560]{1,0:T(8,128)(2,1)} %bitcast.7, bf16[256,2560]{1,0:T(8,128)(2,1)} %weight_hbm.1, bf16[4,256,256]{2,1,0:T(8,128)(2,1)S(1)} %copy-done.1, ...), custom_call_target="tpu_custom_call" | custom-call | flops 10737418240 | bytes 6815744 | tf_op jit(solution)/shard_map/pallas_call | solution.py:512
  179.6 0.0 copy-start.2
  179.6 1.1 copy.10
  180.7 0.7 copy-done.2
  181.4 1.1 copy.11
Async XLA Ops:
  0.6 0.7 copy-start
  1.3 1.0 copy-start.1
  179.6 1.8 copy-start.2

commit v4 on v3

--- a/solution.py
+++ b/solution.py
@@ -35,18 +35,17 @@
 )
 BATCHES = ((0, 512), (2048, 128))
 ORDER = (
-    ("tokens", 4), ("tokens", 3), ("inputs", 0), ("half", 0), ("far", 6), ("tokens", 9),
-    ("half", 1), ("inputs", 1), ("near", 6), ("merge", 6), ("tokens", 2), ("quarter", 0),
-    ("exchange", 4), ("exchange", 3), ("exchange", 9), ("tokens", 5), ("tokens", 7),
-    ("quarter", 1), ("turn", 4), ("tokens", 8), ("tokens", 10), ("exchange", 2), ("turn", 6),
-    ("turn", 3), ("relay", 4), ("turn", 9), ("turn", 0), ("relay", 3), ("relay", 9),
-    ("exchange", 5), ("finish", 4), ("exchange", 7), ("turn", 2), ("relay", 0), ("finish", 3),
-    ("finish", 9), ("turn", 1), ("relay", 2), ("exchange", 8), ("exchange", 10), ("turn", 5),
-    ("finish", 0), ("relay", 6), ("relay", 1), ("turn", 7), ("relay", 5), ("turn", 8),
-    ("finish", 2), ("finish", 1), ("turn", 10), ("relay", 7), ("finish", 6), ("finish", 5),
-    ("relay", 8), ("pack", 0), ("relay", 10), ("decode", 0), ("finish", 8), ("finish", 7),
-    ("finish", 10), ("pack", 1), ("spread", 0), ("decode", 1), ("spread", 1), ("gather", 0),
-    ("gather", 1),
+    ("tokens", 5), ("inputs", 0), ("half", 1), ("far", 6), ("near", 6), ("half", 0),
+    ("tokens", 4), ("tokens", 3), ("inputs", 1), ("merge", 6), ("quarter", 1), ("exchange", 5),
+    ("exchange", 4), ("exchange", 3), ("tokens", 2), ("quarter", 0), ("turn", 5), ("tokens", 9),
+    ("tokens", 7), ("turn", 6), ("turn", 4), ("relay", 5), ("turn", 1), ("tokens", 10),
+    ("tokens", 8), ("relay", 4), ("exchange", 2), ("turn", 3), ("finish", 5), ("finish", 4),
+    ("turn", 0), ("relay", 1), ("exchange", 9), ("relay", 3), ("exchange", 7), ("turn", 2),
+    ("relay", 6), ("relay", 0), ("turn", 9), ("exchange", 10), ("relay", 2), ("finish", 1),
+    ("exchange", 8), ("turn", 7), ("finish", 6), ("finish", 3), ("finish", 0), ("turn", 10),
+    ("finish", 2), ("pack", 0), ("relay", 7), ("relay", 9), ("turn", 8), ("relay", 10),
+    ("relay", 8), ("finish", 7), ("decode", 0), ("finish", 9), ("finish", 10), ("finish", 8),
+    ("pack", 1), ("spread", 0), ("decode", 1), ("spread", 1), ("gather", 0), ("gather", 1),
 )
 
 
@@ -404,20 +403,17 @@
             fresh = weight[:, columns].astype(F32) - (step_rate / REPS) * update
             tile[:, columns] = fresh.astype(BF16)
         own = tile_of(new_weight_ref, batch, rep)
-        send(tile, own, tile_sems, (batch, 0), (twin, member))
         if batch == 0:
+            send(tile, own, tile_sems, (batch, 0), (twin, member))
             send(tile, own, tile_sems, (batch, 1), (rep + 2 - 4 * place_z, member))
             for by in range(1, 4):
                 send(tile, own, tile_sems, (batch, 1 + by), (lax.rem(rep + 4 * by, REPS), member))
         else:
-            for by in range(1, 8):
-                target = lax.rem(chip + by, 8) * 2 + core
-                send(tile, own, tile_sems, (batch, by), (target, member))
+            for by in range(1, REPS):
+                send(tile, own, tile_sems, (batch, by), (peer(by), member))
         own[...] = tile[...]
 
-    def sources(batch, of_core):
-        if batch == 1:
-            return [(by, lax.rem(chip + 8 - by, 8) * 2 + of_core) for by in range(1, 8)]
+    def sources(of_core):
         found = [(1, place_x * 4 + (1 - place_z) * 2 + of_core)]
         for shift, level in ((1, place_z), (4, 1 - place_z)):
             for by in range(1, 4):
@@ -426,20 +422,26 @@
         return found
 
     def stage_spread(batch):
-        for number, owner in sources(batch, core):
+        if batch == 1:
+            for by in range(1, REPS):
+                part = tile_of(new_weight_ref, batch, lax.rem(rep + REPS - by, REPS))
+                arrived(part, tile_sems, (batch, by))
+            return
+        for number, owner in sources(core):
             part = tile_of(new_weight_ref, batch, owner)
             arrived(part, tile_sems, (batch, number))
             send(part, part, tile_sems, (batch, number + 7), (twin, member))
-            if batch == 0 and number == 1:
+            if number == 1:
                 for by in range(1, 4):
                     target = lax.rem(rep + 4 * by, REPS)
                     send(part, part, tile_sems, (batch, 4 + by), (target, member))
 
     def stage_gather(batch):
-        arrived(tile_of(new_weight_ref, batch, twin), tile_sems, (batch, 0))
-        for number, owner in sources(batch, 1 - core):
-            part = tile_of(new_weight_ref, batch, owner)
-            arrived(part, tile_sems, (batch, number + 7))
+        if batch == 0:
+            arrived(tile_of(new_weight_ref, batch, twin), tile_sems, (batch, 0))
+            for number, owner in sources(1 - core):
+                part = tile_of(new_weight_ref, batch, owner)
+                arrived(part, tile_sems, (batch, number + 7))
 
     ready = set()
 
@@ -507,7 +509,7 @@
 def shards(tokens, out_grads, weight, momentum, kept_blocks):
     numbers = kept_blocks[0].transpose(0, 2, 1)
     vmem = pl.BlockSpec(memory_space=pltpu.VMEM)
-    hbm = pl.BlockSpec(memory_space=pl.ANY)
+    hbm = pl.BlockSpec(memory_space=pltpu.HBM)
     dma = pltpu.SemaphoreType.DMA
     new_weight, new_momentum = pl.pallas_call(
         step_kernel,

time: 183 us -> 182 us (level)
  no operation moved by 1% of the time
where the time goes in v4:
time: 182 us
  Pallas kernels  177 us (97%)
  local copies, waits for them, and re-layouts  4.57 us (3%)
    pallas_call x1, Pallas kernels, shards(): pl.pallas_call(step_kernel, out_shape=(jax.ShapeDtypeStruct((ROWS, D), BF...  177 us
    unnamed x8, local copies, waits for them, and re-layouts  4.57 us

profile of v4, /device:TPU:1, one launch (start us, length us, event | category | flops | bytes accessed | tf_op | source)
XLA Modules:
  0.0 182.1 jit_solution(3794800725707445185)
XLA Ops:
  0.6 0.0 copy-start
  0.6 0.7 copy-done
  1.3 0.0 copy-start.1
  1.3 1.0 copy-done.1
  2.4 176.9 %shard_map.77 = (bf16[256,2560]{1,0:T(8,128)(2,1)S(1)}, bf16[256,2560]{1,0:T(8,128)(2,1)}) custom-call(bf16[512,4096]{1,0:T(8,128)(2,1)} %g_hbm.1, bf16[512,2560]{1,0:T(8,128)(2,1)} %t_hbm.1, bf16[256,2560]{1,0:T(8,128)(2,1)} %bitcast.7, bf16[256,2560]{1,0:T(8,128)(2,1)} %weight_hbm.1, bf16[4,256,256]{2,1,0:T(8,128)(2,1)S(1)} %copy-done.1, ...), custom_call_target="tpu_custom_call" | custom-call | flops 10737418240 | bytes 6815744 | tf_op jit(solution)/shard_map/pallas_call | solution.py:514
  179.3 0.0 copy-start.2
  179.3 1.1 copy.10
  180.3 0.7 copy-done.2
  181.0 1.1 copy.11
Async XLA Ops:
  0.6 0.7 copy-start
  1.3 1.0 copy-start.1
  179.3 1.8 copy-start.2

commit v5 on v4

--- a/solution.py
+++ b/solution.py
@@ -35,23 +35,24 @@
 )
 BATCHES = ((0, 512), (2048, 128))
 ORDER = (
-    ("tokens", 5), ("inputs", 0), ("half", 1), ("far", 6), ("near", 6), ("half", 0),
-    ("tokens", 4), ("tokens", 3), ("inputs", 1), ("merge", 6), ("quarter", 1), ("exchange", 5),
-    ("exchange", 4), ("exchange", 3), ("tokens", 2), ("quarter", 0), ("turn", 5), ("tokens", 9),
-    ("tokens", 7), ("turn", 6), ("turn", 4), ("relay", 5), ("turn", 1), ("tokens", 10),
-    ("tokens", 8), ("relay", 4), ("exchange", 2), ("turn", 3), ("finish", 5), ("finish", 4),
-    ("turn", 0), ("relay", 1), ("exchange", 9), ("relay", 3), ("exchange", 7), ("turn", 2),
-    ("relay", 6), ("relay", 0), ("turn", 9), ("exchange", 10), ("relay", 2), ("finish", 1),
-    ("exchange", 8), ("turn", 7), ("finish", 6), ("finish", 3), ("finish", 0), ("turn", 10),
-    ("finish", 2), ("pack", 0), ("relay", 7), ("relay", 9), ("turn", 8), ("relay", 10),
-    ("relay", 8), ("finish", 7), ("decode", 0), ("finish", 9), ("finish", 10), ("finish", 8),
-    ("pack", 1), ("spread", 0), ("decode", 1), ("spread", 1), ("gather", 0), ("gather", 1),
+    ("far", 6), ("tokens", 4), ("tokens", 5), ("tokens", 2), ("near", 6), ("half", 0),
+    ("inputs", 0), ("inputs", 1), ("half", 1), ("merge", 6), ("quarter", 0), ("exchange", 4),
+    ("exchange", 5), ("exchange", 2), ("tokens", 3), ("quarter", 1), ("turn", 4), ("tokens", 9),
+    ("tokens", 7), ("turn", 6), ("turn", 5), ("relay", 4), ("turn", 0), ("tokens", 8),
+    ("tokens", 10), ("relay", 5), ("exchange", 3), ("turn", 2), ("finish", 4), ("relay", 0),
+    ("finish", 5), ("turn", 1), ("exchange", 9), ("relay", 2), ("exchange", 7), ("turn", 3),
+    ("relay", 6), ("relay", 1), ("finish", 0), ("turn", 9), ("exchange", 8), ("relay", 3),
+    ("exchange", 10), ("turn", 7), ("finish", 6), ("relay", 9), ("finish", 2), ("finish", 1),
+    ("turn", 8), ("finish", 3), ("pack", 0), ("relay", 7), ("turn", 10), ("relay", 8),
+    ("finish", 9), ("relay", 10), ("decode", 0), ("finish", 7), ("finish", 8), ("finish", 10),
+    ("pack", 1), ("pass", 0), ("decode", 1), ("spread", 0), ("spread", 1), ("gather", 0),
+    ("gather", 1),
 )
 
 
 NEEDS = {
-    "half": (0, 1), "quarter": (2,), "exchange": (0,), "turn": (3,), "far": (), "near": (),
-    "merge": (),
+    "half": ((0, 1), ()), "quarter": ((2,), ()), "exchange": ((0,), ()), "turn": ((3,), (0,)),
+    "far": ((), (2,)), "near": ((), (1, -1)), "merge": ((), (1, -1)),
 }
 
 
@@ -115,6 +116,7 @@
     groups = (other_mate, SIDE - 1 - mate, mate, pos["y"])
 
     loads = {}
+    ready = set()
 
     def load(name, number, src, dst):
         loads[name] = pltpu.make_async_copy(src, dst, load_sem.at[number])
@@ -143,13 +145,14 @@
     for by in range(1, REPS):
         pl.semaphore_signal(barrier, inc=1, device_id=(peer(by), member), device_id_type=MESH)
 
-    def transpose(block):
-        group = groups[block]
-        loads[block].wait()
-
-        for part in range(SIDE):
-            start = pl.multiple_of(group * 1024 + part * ROWS, ROWS)
-            gt[pl.ds(start, ROWS), :] = stage[block, :, part * ROWS : part * ROWS + ROWS].T
+    def transpose(block, by):
+        if block not in ready:
+            ready.add(block)
+            loads[block].wait()
+        part = turn(pos["z"], by)
+        rows = pl.ds(pl.multiple_of(groups[block] * 1024 + part * ROWS, ROWS), ROWS)
+        columns = pl.ds(pl.multiple_of(part * ROWS, ROWS), ROWS)
+        gt[rows, :] = stage[block, :, columns].T
 
     def partial(axis, group, other, column, width):
         owner = group * SIDE + other if axis == "y" else other * SIDE + group
@@ -427,14 +430,19 @@
                 part = tile_of(new_weight_ref, batch, lax.rem(rep + REPS - by, REPS))
                 arrived(part, tile_sems, (batch, by))
             return
-        for number, owner in sources(core):
+        for number, owner in sources(core)[1:]:
             part = tile_of(new_weight_ref, batch, owner)
             arrived(part, tile_sems, (batch, number))
             send(part, part, tile_sems, (batch, number + 7), (twin, member))
-            if number == 1:
-                for by in range(1, 4):
-                    target = lax.rem(rep + 4 * by, REPS)
-                    send(part, part, tile_sems, (batch, 4 + by), (target, member))
+
+    def stage_pass(batch):
+        number, owner = sources(core)[0]
+        part = tile_of(new_weight_ref, batch, owner)
+        arrived(part, tile_sems, (batch, number))
+        for by in range(1, 4):
+            target = lax.rem(rep + 4 * by, REPS)
+            send(part, part, tile_sems, (batch, 4 + by), (target, member))
+        send(part, part, tile_sems, (batch, number + 7), (twin, member))
 
     def stage_gather(batch):
         if batch == 0:
@@ -443,17 +451,21 @@
                 part = tile_of(new_weight_ref, batch, owner)
                 arrived(part, tile_sems, (batch, number + 7))
 
-    ready = set()
-
     def prepare(name, which):
         needs = []
+        every = (2, 1, -1, 0)
         if name in NEEDS:
-            needs = list(range(SIDE) if JOBS[which][0] == "z" else NEEDS[name])
+            blocks, turns = NEEDS[name]
+            if JOBS[which][0] == "z":
+                blocks = range(SIDE)
+            else:
+                turns = every
+            needs = [(block, by) for block in blocks for by in turns]
             needs += ["t1" if JOBS[which][1] >= 512 else "t0"]
             if JOBS[which][0] == "e":
                 needs += {"exchange": ["g0"], "turn": ["g1"]}[name]
         elif name == "inputs":
-            needs = [1 + which]
+            needs = [(1 + which, by) for by in every]
         elif name == "tokens":
             needs = ["t1"]
         elif name == "finish":
@@ -462,8 +474,8 @@
             if need in ready:
                 continue
             ready.add(need)
-            if need in range(SIDE):
-                transpose(need)
+            if isinstance(need, tuple):
+                transpose(*need)
             elif need in ("g0", "g1"):
                 number = int(need[1])
                 arrived(gp.at[number], pair_sems, (number,))
@@ -475,13 +487,13 @@
         "quarter": stage_quarter, "exchange": stage_exchange,
         "far": lambda job: stage_outward(job, 0), "near": lambda job: stage_outward(job, 1),
         "merge": stage_merge, "turn": stage_turn, "relay": stage_relay, "finish": stage_finish,
-        "pack": stage_pack, "decode": stage_decode, "spread": stage_spread,
+        "pack": stage_pack, "decode": stage_decode, "spread": stage_spread, "pass": stage_pass,
         "gather": stage_gather,
     }
     own_ref[...] = jnp.zeros_like(own_ref)
     for a in range(4):
         own_ref[8 * a : 8 * a + 4, :40] = kept_ref[a]
-    prepare("inputs", 0)
+    prepare("far", 6)
     pl.semaphore_wait(barrier, 4 + REPS - 1)
     for number, (name, which) in enumerate(ORDER):
         if number == 8:

time: 182 us -> 178 us (0.978)
  Pallas kernels: 177 us -> 172 us
    pallas_call x1, Pallas kernels: 177 us -> 172 us  [shards(): pl.pallas_call(step_kernel, out_shape=(jax.ShapeDtypeStruct((ROWS, D), BF...]
where the time goes in v5:
time: 178 us; the launch traced here: 177 us
  Pallas kernels  172 us (97%)
  local copies, waits for them, and re-layouts  4.57 us (3%)
    pallas_call x1, Pallas kernels, shards(): pl.pallas_call(step_kernel, out_shape=(jax.ShapeDtypeStruct((ROWS, D), BF...  172 us
    unnamed x8, local copies, waits for them, and re-layouts  4.57 us

profile of v5, /device:TPU:1, one launch (start us, length us, event | category | flops | bytes accessed | tf_op | source)
XLA Modules:
  0.0 177.3 jit_solution(2416941385516533586)
XLA Ops:
  0.6 0.0 copy-start
  0.6 0.7 copy-done
  1.3 0.0 copy-start.1
  1.3 1.0 copy-done.1
  2.4 172.1 %shard_map.77 = (bf16[256,2560]{1,0:T(8,128)(2,1)S(1)}, bf16[256,2560]{1,0:T(8,128)(2,1)}) custom-call(bf16[512,4096]{1,0:T(8,128)(2,1)} %g_hbm.1, bf16[512,2560]{1,0:T(8,128)(2,1)} %t_hbm.1, bf16[256,2560]{1,0:T(8,128)(2,1)} %bitcast.7, bf16[256,2560]{1,0:T(8,128)(2,1)} %weight_hbm.1, bf16[4,256,256]{2,1,0:T(8,128)(2,1)S(1)} %copy-done.1, ...), custom_call_target="tpu_custom_call" | custom-call | flops 10737418240 | bytes 6815744 | tf_op jit(solution)/shard_map/pallas_call | solution.py:526
  174.5 0.0 copy-start.2
  174.5 1.1 copy.10
  175.5 0.7 copy-done.2
  176.3 1.1 copy.11
Async XLA Ops:
  0.6 0.7 copy-start
  1.3 1.0 copy-start.1
  174.5 1.8 %copy-start.2 = (bf16[256,2560]{1,0:T(8,128)(2,1)S(1)}, bf16[256,2560]{1,0:T(8,128)(2,1)}, u32[]{:S(2)}) copy-start(bf16[256,2560]{1,0:T(8,128)(2,1)} %get-tuple-element.5) | copy-start | bytes 3932164

commit v6 on v5

--- a/solution.py
+++ b/solution.py
@@ -76,9 +76,9 @@
 
 
 def step_kernel(
-    g_hbm, t_hbm, mom_hbm, weight_hbm, table_hbm, kept_ref,
+    g_hbm, t_hbm, mom_hbm, weight_hbm, table_hbm, kept_hbm,
     new_weight_ref, new_mom_ref,
-    gt, gp, stage, tokens, tp, own_ref, mom, grad, table, weight0, weight1,
+    gt, gp, stage, tokens, tp, kept_ref, own_ref, mom, grad, table, weight0, weight1,
     picked, packed, packed_in, kept_in, tile0, tile1, values, numbers_in,
     load_sem, send_sem, recv_sem, pair_send, pair_recv, kept_send, kept_recv, pack_send, pack_recv,
     tile_send, tile_recv, *bufs,
@@ -130,6 +130,7 @@
     load("t0", 4, t_hbm.at[:, :512], tokens.at[:, :512])
     for block in range(1, SIDE):
         load_group(block)
+    load("kept", 10, kept_hbm, kept_ref)
     load("t1", 5, t_hbm.at[:, 512:], tokens.at[:, 512:])
     load("mom", 6, mom_hbm, mom)
     load("table", 7, table_hbm, table)
@@ -491,6 +492,7 @@
         "gather": stage_gather,
     }
     own_ref[...] = jnp.zeros_like(own_ref)
+    loads["kept"].wait()
     for a in range(4):
         own_ref[8 * a : 8 * a + 4, :40] = kept_ref[a]
     prepare("far", 6)
@@ -529,7 +531,7 @@
             jax.ShapeDtypeStruct((ROWS, D), BF16),
             jax.ShapeDtypeStruct((ROWS, D), BF16),
         ),
-        in_specs=[hbm] * 5 + [vmem],
+        in_specs=[hbm] * 6,
         out_specs=(vmem, vmem),
         scratch_shapes=[
             pltpu.VMEM((4096, 512), BF16),
@@ -537,6 +539,7 @@
             pltpu.VMEM((SIDE, 512, 1024), BF16),
             pltpu.VMEM((512, D), BF16),
             pltpu.VMEM((512, D), BF16),
+            pltpu.VMEM((4, 4, 40), jnp.int32),
             pltpu.VMEM((32, 128), jnp.int32),
             pltpu.VMEM((ROWS, D), BF16),
             pltpu.VMEM((ROWS, D), F32),
@@ -551,7 +554,7 @@
             pltpu.VMEM((64, 128), BF16),
             pltpu.VMEM((REPS * 32, 512), F32),
             pltpu.VMEM((REPS * 8, 512), jnp.int32),
-            dma((10,)),
+            dma((11,)),
             dma((len(JOBS), 2, 6)),
             dma((len(JOBS), 2, 6)),
             dma((2 + len(JOBS),)),
@@ -569,7 +572,7 @@
         ]
         + [pltpu.VMEM((2 if kind == "z" else 1, 6, ROWS, width), BF16) for kind, _, width in JOBS],
         compiler_params=pltpu.CompilerParams(
-            collective_id=0, has_side_effects=True, vmem_limit_bytes=52 * 2**20
+            collective_id=0, has_side_effects=True, vmem_limit_bytes=49 * 2**20
         ),
         cost_estimate=pl.CostEstimate(
             flops=2 * 512 * 4096 * D, bytes_accessed=2 * 512 * (4096 + D), transcendentals=0

time: 178 us -> 177 us (level)
  Pallas kernels: 172 us -> 170 us
where the time goes in v6:
time: 177 us; the launch traced here: 176 us
  Pallas kernels  170 us (96%)
  local copies, waits for them, and re-layouts  5.16 us (3%)
    pallas_call x1, Pallas kernels, shards(): pl.pallas_call(step_kernel, out_shape=(jax.ShapeDtypeStruct((ROWS, D), BF...  170 us
    unnamed x8, local copies, waits for them, and re-layouts  5.16 us

profile of v6, /device:TPU:1, one launch (start us, length us, event | category | flops | bytes accessed | tf_op | source)
XLA Modules:
  0.0 176.3 jit_solution(4338305347666627335)
XLA Ops:
  0.6 0.0 copy-start
  0.6 1.3 copy-done
  1.9 0.0 copy-start.1
  2.0 0.7 copy-done.1
  2.6 0.0 copy-start.2
  2.6 1.0 copy-done.2
  3.7 170.5 %shard_map.77 = (bf16[256,2560]{1,0:T(8,128)(2,1)S(1)}, bf16[256,2560]{1,0:T(8,128)(2,1)S(1)}) custom-call(bf16[512,4096]{1,0:T(8,128)(2,1)} %g_hbm.1, bf16[512,2560]{1,0:T(8,128)(2,1)} %t_hbm.1, bf16[256,2560]{1,0:T(8,128)(2,1)S(1)} %bitcast.6, bf16[256,2560]{1,0:T(8,128)(2,1)} %weight_hbm.1, bf16[4,256,256]{2,1,0:T(8,128)(2,1)S(1)} %copy-done.2, ...), custom_call_target="tpu_custom_call" | custom-call | flops 10737418240 | bytes 6815744 | tf_op jit(solution)/shard_map/pallas_call | solution.py:528
  174.2 1.1 copy.10
  175.3 1.1 copy.11
Async XLA Ops:
  0.6 1.3 copy-start
  1.9 0.7 copy-start.1
  2.6 1.0 copy-start.2
